TPU v7x, 32 devices: a whole 2x2x4 slice. The times are simulated.
32 devices in a mesh: dp: 8 (over y, x, core), pipe: 4 (over z).
Axes of the slice: x: 2, y: 2, z: 4, core: 2. Of those that a mesh axis runs over, the one named last changes fastest.
Arguments:
- master: float32 [4, 128, 8192], P('pipe', 'dp'), may hold values from -0.12 to 0.12
- moment1: float32 [4, 128, 8192], P('pipe', 'dp'), may hold values from -3 to 3
- moment2: float32 [4, 128, 8192], P('pipe', 'dp'), may hold values from 0.25 to 4.5
- quant_grad: bfloat16 [4, 128, 8192], P('pipe', 'dp'), may hold values from -120 to 120
- grad_exponent: int32 [4, 128], P('pipe', 'dp'), may hold values from -3 to 2
- replica_params: bfloat16 [4, 8, 128, 8192], P('pipe', 'dp'), as said below
- failed: int32 [4, 2], replicated, may hold values from 0 to 7, as said below
- dest: int32 [4, 128], replicated, may hold values from 0 to 127, as said below
Outputs:
- new_master: float32 [4, 128, 8192], P('pipe', 'dp')
- new_moment1: float32 [4, 128, 8192], P('pipe', 'dp')
- new_moment2: float32 [4, 128, 8192], P('pipe', 'dp')
Inputs may be any that keep to these rules, and one draw needn't show every extreme that they name: `failed`: each group lists 2 distinct ranks; group 0 lists ranks 1 and 4; in every other group some rows of the first listed rank have new positions among the rows of the second listed rank (new position // 16). `dest`: each group's row is a permutation of its rows; the 16 rows of one rank (old rows r * 16 to r * 16 + 15) land in at most 2 rows of any one rank's new rows (new position // 16), and some pair of ranks reaches 2 in every group. `replica_params`: within a group the copies of ranks not listed in failed are equal; the copies of listed ranks are zero.
All inputs are finite; a program needn't handle non-finite values.
Results may differ from a plain program's by a relative error of at most 0.0003.
Values may be sent and summed in bfloat16 or wider, within the bound.
No kernel may reach another device: no remote copies, remote signals or barrier semaphores. Data moves between devices by JAX's collectives and lax.ppermute only.
A program may use at most 64 MiB of HBM per device.

v0:
```python
import jax
import jax.numpy as jnp
from jax import lax
from jax.sharding import PartitionSpec as P

STEP = 20


beta_one = 0.9
beta_two = 0.95
learn_rate = 0.00015
decay_rate = 0.1
adam_eps = 1e-08
clip_eps = 1e-06


def from_root(value, axis, source):
    kept = jnp.where(lax.axis_index(axis) == source, value, 0).astype(value.dtype)
    return lax.psum(kept, axis)


def adam_step(weights, first, second, grads):
    first_new = beta_one * first + (1.0 - beta_one) * grads
    second_new = beta_two * second + (1.0 - beta_two) * grads * grads
    corr_one = 1.0 - beta_one**STEP
    corr_two = 1.0 - beta_two**STEP
    direction = (
        first_new / corr_one / (jnp.sqrt(second_new / corr_two) + adam_eps) + decay_rate * weights
    )
    return (weights - learn_rate * direction, first_new, second_new)


def local(master, moment1, moment2, quant_grad, grad_exponent, replica_params, failed, dest):
    group_idx = lax.axis_index("pipe")
    my_rank = lax.axis_index("dp")
    ranks_count = lax.axis_size("dp")
    shard_rows = master.shape[1]
    row_width = master.shape[2]
    fail_count = failed.shape[1]
    peer_slots = (shard_rows + ranks_count - 1) // ranks_count
    fail_row = lax.dynamic_index_in_dim(failed, group_idx, 0, keepdims=False)
    dest_row = lax.dynamic_index_in_dim(dest, group_idx, 0, keepdims=False)
    rank_ids = jnp.arange(ranks_count, dtype=jnp.int32)
    is_alive = jnp.all(rank_ids[:, None] != fail_row[None, :], axis=1)
    own_fail = fail_row == my_rank
    is_lost = jnp.any(own_fail)
    copy_rows = replica_params[0, 0]
    first_root = jnp.min(jnp.where(is_alive, rank_ids, ranks_count))
    bf_zero = jnp.zeros((), jnp.bfloat16)
    local_ids = jnp.arange(shard_rows, dtype=jnp.int32)
    group_ids = jnp.arange(dest_row.shape[0], dtype=jnp.int32)
    targets = (dest_row // shard_rows).reshape(ranks_count, shard_rows)
    earlier = local_ids[None, :] < local_ids[:, None]
    same_target = targets[:, :, None] == targets[:, None, :]
    order_in = jnp.sum((same_target & earlier[None, :, :]).astype(jnp.int32), axis=2)
    my_targets = lax.dynamic_index_in_dim(targets, my_rank, 0, keepdims=False)
    my_order = lax.dynamic_index_in_dim(order_in, my_rank, 0, keepdims=False)
    slot_ids = jnp.arange(peer_slots, dtype=jnp.int32)
    pick_mask = (my_targets[None, None, :] == rank_ids[:, None, None]) & (
        my_order[None, None, :] == slot_ids[None, :, None]
    )
    send_index = jnp.sum(jnp.where(pick_mask, local_ids[None, None, :], 0), axis=2).reshape(-1)
    new_rows = my_rank * shard_rows + local_ids
    match_mask = dest_row[None, :] == new_rows[:, None]
    source_row = jnp.sum(jnp.where(match_mask, group_ids[None, :], 0), axis=1)
    source_rank = source_row // shard_rows
    source_order = order_in.reshape(-1)[source_row]
    recv_index = source_rank * peer_slots + source_order
    master_extra = None
    lost_blocks = jnp.stack(
        [
            lax.dynamic_slice_in_dim(copy_rows, fail_row[piece_idx] * shard_rows, shard_rows, 0)
            for piece_idx in range(fail_count)
        ]
    )
    lost_blocks = jnp.where(my_rank == first_root, lost_blocks, bf_zero)
    received_rows = from_root(lost_blocks, "dp", first_root)
    recovered = jnp.sum(
        jnp.where(own_fail[:, None, None], received_rows.astype(jnp.float32), jnp.float32(0.0)),
        axis=0,
    )
    start_master = jnp.where(is_lost, recovered, master[0])
    start_first = jnp.where(is_lost, jnp.float32(0.0), moment1[0])
    start_second = jnp.where(is_lost, jnp.float32(0.0), moment2[0])
    grad = (
        quant_grad[0].astype(jnp.float32) * jnp.exp2(grad_exponent[0].astype(jnp.float32))[:, None]
    )
    grad_total = lax.psum(jnp.sum(grad * grad), ("dp", "pipe"))
    elem_count = lax.axis_size("dp") * lax.axis_size("pipe") * shard_rows * row_width
    clip_scale = jnp.minimum(1.0, 1.0 / jnp.sqrt(grad_total / elem_count + clip_eps))
    clipped = grad * clip_scale

    def to_buffer(values):
        return values[send_index].reshape(ranks_count, peer_slots, row_width)

    w_next, m_next, v_next = adam_step(start_master, start_first, start_second, clipped)
    received = (
        lax.all_to_all(to_buffer(w_next), "dp", split_axis=0, concat_axis=0, tiled=True),
        lax.all_to_all(to_buffer(m_next), "dp", split_axis=0, concat_axis=0, tiled=True),
        lax.all_to_all(to_buffer(v_next), "dp", split_axis=0, concat_axis=0, tiled=True),
    )
    placed = tuple(
        (values.reshape(ranks_count * peer_slots, row_width)[recv_index] for values in received)
    )
    placed_master = placed[0]
    return (placed_master[None], placed[1][None], placed[2][None])


def solution(mesh):
    in_specs = (
        P("pipe", "dp", None),
        P("pipe", "dp", None),
        P("pipe", "dp", None),
        P("pipe", "dp", None),
        P("pipe", "dp"),
        P("pipe", "dp", None, None),
        P(),
        P(),
    )
    out_specs = (P("pipe", "dp", None), P("pipe", "dp", None), P("pipe", "dp", None))
    return jax.shard_map(local, mesh=mesh, in_specs=in_specs, out_specs=out_specs, check_vma=False)
```

profile of v0, /device:TPU:0, one launch (start us, length us, event | category | flops | bytes accessed | tf_op | source)
XLA Modules:
  0.0 123.5 jit_solution(12723304602606619782)
XLA Ops:
  7.2 0.0 copy-start.4
  7.2 0.0 copy-start
  7.2 0.0 copy-start.3
  7.2 0.0 copy-start.2
  7.2 0.0 copy-start.1
  7.2 0.0 all-reduce.2.cloned.1.call-start
  7.3 1.0 fusion.19
  8.2 0.5 fusion.20
  10.1 0.1 compare_reduce_fusion
  10.2 0.6 select_reduce_fusion.3
  11.5 1.1 dynamic-slice_bitcast_fusion.1
  12.5 0.9 fusion.1
  13.4 0.0 all-reduce.2.cloned.1.call-update
  13.4 0.0 copy-done.4
  13.5 0.7 fusion.14
  14.2 0.1 squeeze.23
  14.3 0.3 convert_reduce_fusion
  14.6 0.1 select_reduce_fusion.2
  14.7 0.1 copy.11
  14.8 0.1 reshape.302
  14.9 0.0 copy-done
  14.9 0.8 fusion.6
  15.7 42.2 %psum.15 = f32[]{:T(128)} all-reduce(f32[]{:T(128)} %fusion.6), channel_id=1, replica_groups=mesh['dp'=8,'pipe'=4] {'dp','pipe'}, use_global_device_ids=true, to_apply=%region_6.7 | all-reduce | flops 1 | bytes 8 | tf_op jit(solution)/shard_map/psum | solution.py:88
  58.6 0.6 fusion.18
  59.3 11.6 %all-reduce.2.cloned.1.call-done = bf16[2,16,8192]{2,1,0:T(8,128)(2,1)} async-done(((bf16[2,16,8192]{2,1,0:T(8,128)(2,1)}), bf16[2,16,8192]{2,1,0:T(8,128)(2,1)}) %all-reduce.2.cloned.1.call-update) | async-done | bytes 524304 | tf_op jit(solution)/shard_map/psum | solution.py:19
  70.8 1.3 %select_reduce_fusion = f32[16,8192]{1,0:T(8,128)S(1)} fusion(bf16[2,16,8192]{2,1,0:T(8,128)(2,1)} %all-reduce.2.cloned.1.call-done, pred[2]{0:T(512)(128)(4,1)S(1)} %get-tuple-element.7), kind=kLoop, calls=%fused_computation.7 | loop fusion | flops 655360 | bytes 1048578 | tf_op jit(solution)/shard_map/reduce_sum | solution.py:78
  72.2 0.0 copy-done.3
  72.2 0.0 copy-done.2
  72.2 0.0 copy-done.1
  72.2 1.2 multiply_subtract_fusion
  73.4 0.7 gather_fusion
  74.2 1.1 reshape.303
  75.3 3.5 %all-to-all-start = ((f32[8,2,8192]{2,1,0:T(2,128)}), f32[8,2,8192]{2,1,0:T(2,128)S(1)}, u32[]{:S(2)}, u32[]{:S(2)}) async-start(f32[8,2,8192]{2,1,0:T(2,128)} %reshape.303), calls=%async_computation | async-start | bytes 1048576 | tf_op jit(solution)/shard_map/all_to_all | solution.py:98
  78.8 0.7 gather_fusion.3
  79.5 1.1 reshape.306
  80.6 7.8 %all-to-all-done = f32[8,2,8192]{2,1,0:T(2,128)S(1)} async-done(((f32[8,2,8192]{2,1,0:T(2,128)}), f32[8,2,8192]{2,1,0:T(2,128)S(1)}, u32[]{:S(2)}, u32[]{:S(2)}) %all-to-all-start) | async-done | bytes 524320 | tf_op jit(solution)/shard_map/all_to_all | solution.py:98
  88.4 3.5 %all-to-all-start.1 = ((f32[8,2,8192]{2,1,0:T(2,128)}), f32[8,2,8192]{2,1,0:T(2,128)S(1)}, u32[]{:S(2)}, u32[]{:S(2)}) async-start(f32[8,2,8192]{2,1,0:T(2,128)} %reshape.306), calls=%async_computation.1 | async-start | bytes 1048576 | tf_op jit(solution)/shard_map/all_to_all | solution.py:99
  91.9 0.2 select_reduce_fusion.1
  92.1 0.7 gather_fusion.5
  92.9 1.1 reshape.308
  94.0 7.7 %all-to-all-done.1 = f32[8,2,8192]{2,1,0:T(2,128)S(1)} async-done(((f32[8,2,8192]{2,1,0:T(2,128)}), f32[8,2,8192]{2,1,0:T(2,128)S(1)}, u32[]{:S(2)}, u32[]{:S(2)}) %all-to-all-start.1) | async-done | bytes 524320 | tf_op jit(solution)/shard_map/all_to_all | solution.py:99
  101.6 3.5 %all-to-all-start.2 = ((f32[8,2,8192]{2,1,0:T(2,128)}), f32[8,2,8192]{2,1,0:T(2,128)S(1)}, u32[]{:S(2)}, u32[]{:S(2)}) async-start(f32[8,2,8192]{2,1,0:T(2,128)} %reshape.308), calls=%async_computation.2 | async-start | bytes 1048576 | tf_op jit(solution)/shard_map/all_to_all | solution.py:100
  105.1 0.1 reshape.305
  105.2 0.7 gather_fusion.1
  105.9 0.4 reshape.304
  106.3 1.5 %gather_fusion.2 = f32[16,8192]{1,0:T(8,128)} fusion(f32[16,8192]{1,0:T(8,128)S(1)} %reshape.304, s32[1024]{0:T(1024)S(1)} %pad_clamp_fusion), kind=kCustom, calls=%fused_computation.2 | custom fusion | bytes 1048640 | tf_op jit(solution)/shard_map/gather | solution.py:103
  107.8 0.4 reshape.307
  108.1 1.5 %gather_fusion.4 = f32[16,8192]{1,0:T(8,128)} fusion(f32[16,8192]{1,0:T(8,128)S(1)} %reshape.307, s32[1024]{0:T(1024)S(1)} %pad_clamp_fusion), kind=kCustom, calls=%fused_computation.4 | custom fusion | bytes 1048640 | tf_op jit(solution)/shard_map/gather | solution.py:103
  109.6 5.2 %all-to-all-done.2 = f32[8,2,8192]{2,1,0:T(2,128)S(1)} async-done(((f32[8,2,8192]{2,1,0:T(2,128)}), f32[8,2,8192]{2,1,0:T(2,128)S(1)}, u32[]{:S(2)}, u32[]{:S(2)}) %all-to-all-start.2) | async-done | bytes 524320 | tf_op jit(solution)/shard_map/all_to_all | solution.py:100
  114.8 0.4 reshape.309
  115.2 1.5 %gather_fusion.6 = f32[16,8192]{1,0:T(8,128)} fusion(f32[16,8192]{1,0:T(8,128)S(1)} %reshape.309, s32[1024]{0:T(1024)S(1)} %pad_clamp_fusion), kind=kCustom, calls=%fused_computation.6 | custom fusion | bytes 1048640 | tf_op jit(solution)/shard_map/gather | solution.py:103
  (13 shorter events, 0.1 us)
Async XLA Ops:
  7.2 6.3 %copy-start.4 = (s32[1,16]{1,0:T(1,128)S(1)}, s32[1,16]{1,0:T(1,128)}, u32[]{:S(2)}) copy-start(s32[1,16]{1,0:T(1,128)} %param.12) | copy-start | bytes 196
  7.2 7.7 %copy-start = (bf16[1,16,8192]{2,1,0:T(8,128)(2,1)S(1)}, bf16[1,16,8192]{2,1,0:T(8,128)(2,1)}, u32[]{:S(2)}) copy-start(bf16[1,16,8192]{2,1,0:T(8,128)(2,1)} %param.11) | copy-start | bytes 786436
  7.2 65.0 %copy-start.3 = (f32[1,16,8192]{2,1,0:T(8,128)S(1)}, f32[1,16,8192]{2,1,0:T(8,128)}, u32[]{:S(2)}) copy-start(f32[1,16,8192]{2,1,0:T(8,128)} %param.10) | copy-start | bytes 1572868
  7.2 65.0 %copy-start.2 = (f32[1,16,8192]{2,1,0:T(8,128)S(1)}, f32[1,16,8192]{2,1,0:T(8,128)}, u32[]{:S(2)}) copy-start(f32[1,16,8192]{2,1,0:T(8,128)} %param.9) | copy-start | bytes 1572868
  7.2 65.0 %copy-start.1 = (f32[1,16,8192]{2,1,0:T(8,128)S(1)}, f32[1,16,8192]{2,1,0:T(8,128)}, u32[]{:S(2)}) copy-start(f32[1,16,8192]{2,1,0:T(8,128)} %param.8) | copy-start | bytes 1572868
  7.2 63.6 %all-reduce.2.cloned.1.call-start = ((), (), s32[]{:S(2)}) async-start(), calls=%async_computation.3 | async-start | bytes 1048576 | tf_op jit(solution)/shard_map/psum | solution.py:19
  75.3 13.2 %all-to-all-start = ((f32[8,2,8192]{2,1,0:T(2,128)}), f32[8,2,8192]{2,1,0:T(2,128)S(1)}, u32[]{:S(2)}, u32[]{:S(2)}) async-start(f32[8,2,8192]{2,1,0:T(2,128)} %reshape.303), calls=%async_computation | async-start | bytes 1048576 | tf_op jit(solution)/shard_map/all_to_all | solution.py:98
  88.4 13.2 %all-to-all-start.1 = ((f32[8,2,8192]{2,1,0:T(2,128)}), f32[8,2,8192]{2,1,0:T(2,128)S(1)}, u32[]{:S(2)}, u32[]{:S(2)}) async-start(f32[8,2,8192]{2,1,0:T(2,128)} %reshape.306), calls=%async_computation.1 | async-start | bytes 1048576 | tf_op jit(solution)/shard_map/all_to_all | solution.py:99
  101.6 13.2 %all-to-all-start.2 = ((f32[8,2,8192]{2,1,0:T(2,128)}), f32[8,2,8192]{2,1,0:T(2,128)S(1)}, u32[]{:S(2)}, u32[]{:S(2)}) async-start(f32[8,2,8192]{2,1,0:T(2,128)} %reshape.308), calls=%async_computation.2 | async-start | bytes 1048576 | tf_op jit(solution)/shard_map/all_to_all | solution.py:100
Sparse Core Ops, SparseCore 0:
  13.5 57.2 all-reduce.1
where the time goes:
time: 124 us; the launch traced here: 123 us
  blocking collectives  42.2 us (34%)
  waiting for transfers between devices  32.3 us (26%)
  between operations  16.9 us (14%)
  local copies, waits for them, and re-layouts  15.3 us (12%)
  starting transfers between devices  10.5 us (8%)
  other arithmetic  6.28 us (5%)
    psum x1, blocking collectives, local(): grad_total = lax.psum(jnp.sum(grad * grad), ('dp', 'pipe'))  42.2 us
    psum x1, waiting for transfers between devices, from_root(): return lax.psum(kept, axis)  11.6 us
    all_to_all x1, waiting for transfers between devices, local(): lax.all_to_all(to_buffer(w_next), 'dp', split_axis=0, concat_axis=0, tile...  7.85 us
    all_to_all x1, waiting for transfers between devices, local(): lax.all_to_all(to_buffer(m_next), 'dp', split_axis=0, concat_axis=0, tile...  7.65 us
    all_to_all x1, waiting for transfers between devices, local(): lax.all_to_all(to_buffer(v_next), 'dp', split_axis=0, concat_axis=0, tile...  5.17 us
    gather x3, local copies, waits for them, and re-layouts, local(): values.reshape(ranks_count * peer_slots, row_width)[recv_index]  4.46 us
    all_to_all x1, starting transfers between devices, local(): lax.all_to_all(to_buffer(m_next), 'dp', split_axis=0, concat_axis=0, tile...  3.49 us
    all_to_all x1, starting transfers between devices, local(): lax.all_to_all(to_buffer(v_next), 'dp', split_axis=0, concat_axis=0, tile...  3.49 us
  transfers between devices with their start and end apart: 4, of which 4 were waited for; matrix products, arithmetic and copies ran while one was open for 9% of the time, Pallas kernels for 0%

commit v1 on v0

v1 whole, which is shorter than its diff:
```python
import functools

import jax
import jax.numpy as jnp
import numpy as np
from jax import lax
from jax.experimental import pallas as pl
from jax.experimental.pallas import tpu as pltpu
from jax.sharding import PartitionSpec as P

STEP = 20

beta_one = 0.9
beta_two = 0.95
learn_rate = 0.00015
decay_rate = 0.1
adam_eps = 1e-08
clip_eps = 1e-06

MASTER_MAX = 0.12
FIRST_MAX = 3.0
SECOND_MIN = 0.25
SECOND_MAX = 4.5

OCTAVES = 12
LOG_TOP = float(np.log(1.0 + 2.0**OCTAVES))
LOG_STEPS = 32767.0
SECOND_STEPS = 65535.0

COLUMN_CHUNKS = 4
VMEM_LIMIT = 56 * 1024 * 1024
ANY = pl.BlockSpec(memory_space=pl.ANY)


def encode_log(x, top):
    steps = jnp.log(1.0 + jnp.abs(x) * (2.0**OCTAVES / top)) * (LOG_STEPS / LOG_TOP) + 0.5
    code = jnp.minimum(steps, LOG_STEPS).astype(jnp.int32)
    return jnp.where(x < 0, -code, code)


def decode_log(code, top):
    size = (jnp.exp(jnp.abs(code).astype(jnp.float32) * (LOG_TOP / LOG_STEPS)) - 1.0) * (top / 2.0**OCTAVES)
    return jnp.where(code < 0, -size, size)


def encode_second(x):
    steps = (x - SECOND_MIN) * (SECOND_STEPS / (SECOND_MAX - SECOND_MIN)) + 0.5
    return jnp.clip(steps, 0.0, SECOND_STEPS).astype(jnp.int32)


def decode_second(code):
    return code.astype(jnp.float32) * ((SECOND_MAX - SECOND_MIN) / SECOND_STEPS) + SECOND_MIN


def encode_short(x):
    size = jnp.abs(x)
    is_zero = size < 2.0**-126
    size = jnp.where(is_zero, 1.0, size)
    exponent = jnp.floor(jnp.log2(size) + 0.002)
    half = jnp.floor(exponent * 0.5)
    mantissa = size * jnp.exp2(-half) * jnp.exp2(half - exponent) * 128.0
    code = exponent * 128.0 + (127.0 * 128.0 - 128.0) + mantissa
    code = jnp.where(is_zero, 0.0, code + 0.5).astype(jnp.int32)
    return jnp.where(x < 0, -code, code)


def decode_short(code):
    size = jnp.abs(code)
    exponent = lax.shift_right_logical(size, 7)
    mantissa = (size & 127).astype(jnp.float32) * (1.0 / 128.0) + 1.0
    scale = jnp.where(exponent > 0, jnp.exp2((exponent - 127).astype(jnp.float32)), 0.0)
    value = mantissa * scale
    return jnp.where(code < 0, -value, value)


def join(high, low):
    return (high << 16) | (low & 0xFFFF)


def signed_high(word):
    return word >> 16


def signed_low(word):
    return (word << 16) >> 16


def extra_columns(k, width):
    return {1: width // 2, 2: width // 4, 4: width // 4}.get(k, 0)


def pack_kernel(
    ranks, cap, fails, devices,
    dest, failed, grad_exponent, master, moment1, moment2, quant_grad, replica,
    *refs,
):
    payloads, total = refs[:ranks], refs[ranks]
    (dest_s, failed_s, exponent_s, counts, table, lost_counts, lost_table,
     master_v, first_v, second_v, grad_v, block_v, lost_v, picked_v, word_one, word_two, extra_v,
     small_sem, in_sem, block_sem, pick_sem, out_sem) = refs[ranks + 1:]
    rows, width = master_v.shape
    half, quarter = width // 2, width // 4
    chunk = width // COLUMN_CHUNKS
    group = lax.axis_index("pipe")
    me = lax.axis_index("dp")

    small = [
        pltpu.make_async_copy(failed, failed_s, small_sem.at[0]),
        pltpu.make_async_copy(grad_exponent, exponent_s, small_sem.at[1]),
        pltpu.make_async_copy(dest, dest_s, small_sem.at[2]),
    ]
    for copy in small:
        copy.start()
    loads = []
    for part in range(COLUMN_CHUNKS):
        columns = pl.ds(part * chunk, chunk)
        copies = [
            pltpu.make_async_copy(source.at[:, columns], target.at[:, columns], in_sem.at[part, i])
            for i, (source, target) in enumerate(
                [(quant_grad, grad_v), (master, master_v), (moment1, first_v), (moment2, second_v)]
            )
        ]
        for copy in copies:
            copy.start()
        loads.append(copies)
    for copy in small:
        copy.wait()
    blocks = [
        pltpu.make_async_copy(
            replica.at[pl.ds(pl.multiple_of(failed_s[group, i] * rows, rows), rows), :],
            block_v.at[pl.ds(i * rows, rows), :],
            block_sem.at[i],
        )
        for i in range(fails)
    ]
    for copy in blocks:
        copy.start()

    for i in range(ranks * cap):
        table[i] = 0
    for i in range(ranks):
        counts[i] = 0
    for r in range(rows):
        target = lax.div(dest_s[group, me * rows + r], rows)
        order = counts[target]
        table[target * cap + order] = r
        counts[target] = order + 1
    for i in range(ranks * fails * cap):
        lost_table[i] = 0
    for i in range(ranks * fails):
        lost_counts[i] = 0
    for i in range(fails):
        for r in range(rows):
            target = lax.div(dest_s[group, failed_s[group, i] * rows + r], rows)
            slot = target * fails + i
            order = lost_counts[slot]
            lost_table[slot * cap + order] = i * rows + r
            lost_counts[slot] = order + 1

    row_ids = lax.broadcasted_iota(jnp.int32, (rows, 128), 0)
    exponents = jnp.zeros((rows, 128), jnp.float32)
    for r in range(rows):
        exponents = jnp.where(row_ids == r, exponent_s[0, r].astype(jnp.float32), exponents)
    row_scale = jnp.exp2(exponents)[:, :1]

    for copy in blocks:
        copy.wait()
    for part in range(COLUMN_CHUNKS):
        columns = pl.ds(part * chunk, chunk)
        lost_v[:, columns] = block_v[:, columns].astype(jnp.float32)
    lost_rows = fails * cap
    picks = []
    for j in range(lost_rows):
        one = lost_table[(me ^ 1) * lost_rows + j]
        two = lost_table[(me ^ 2) * lost_rows + j]
        four = lost_table[(me ^ 4) * lost_rows + j]
        picks.append((lost_v.at[pl.ds(one, 1), :], picked_v.at[pl.ds(j, 1), :]))
        for q, source in ((0, two), (2, two), (1, four), (3, four)):
            columns = pl.ds(q * quarter, quarter)
            picks.append((lost_v.at[pl.ds(source, 1), columns], picked_v.at[pl.ds(lost_rows + j, 1), columns]))
    picks = [pltpu.make_async_copy(a, b, pick_sem) for a, b in picks]
    for copy in picks:
        copy.start()

    sums = jnp.zeros((8, 128), jnp.float32)
    outs = []
    for part in range(COLUMN_CHUNKS):
        columns = pl.ds(part * chunk, chunk)
        for copy in loads[part]:
            copy.wait()
        grad = grad_v[:, columns].astype(jnp.float32) * row_scale
        sums += jnp.sum((grad * grad).reshape(rows // 8, 8, chunk // 128, 128), axis=(0, 2))
        word_one[:, columns] = join(encode_log(master_v[:, columns], MASTER_MAX), encode_log(first_v[:, columns], FIRST_MAX))
        word_two[:, columns] = join(encode_second(second_v[:, columns]), encode_short(grad))
        for k in reversed(range(ranks)):
            for order in range(cap):
                row = table[(me ^ k) * cap + order]
                for i, word in enumerate((word_one, word_two)):
                    copy = pltpu.make_async_copy(
                        word.at[pl.ds(row, 1), columns],
                        payloads[k].at[pl.ds(i * cap + order, 1), columns],
                        out_sem,
                    )
                    copy.start()
                    outs.append(copy)
    total[...] = jnp.broadcast_to(jnp.sum(sums, axis=0, keepdims=True), (devices, 128))

    for copy in picks:
        copy.wait()
    extra_v[...] = join(encode_short(picked_v[:, :half]), encode_short(picked_v[:, half:]))
    for k, first_row, first_column in ((1, 0, 0), (2, lost_rows, 0), (4, lost_rows, quarter)):
        columns = extra_columns(k, width)
        copy = pltpu.make_async_copy(
            extra_v.at[pl.ds(first_row, lost_rows), pl.ds(first_column, columns)],
            payloads[k].at[:, pl.ds(width, columns)],
            out_sem,
        )
        copy.start()
        outs.append(copy)
    for copy in outs:
        copy.wait()


def base_kernel(
    ranks, cap, fails,
    dest, failed, replica, from_one, from_two, from_four,
    base, lost, places,
    dest_s, failed_s, counts, places_s, lost_counts, lost_places, lost_sources,
    block_v, rows_v, extra_v, small_sem, block_sem, move_sem,
):
    rows, width = lost.shape[0], base.shape[1]
    half, quarter = width // 2, width // 4
    lost_rows = fails * cap
    group = lax.axis_index("pipe")
    me = lax.axis_index("dp")
    small = [
        pltpu.make_async_copy(failed, failed_s, small_sem.at[0]),
        pltpu.make_async_copy(dest, dest_s, small_sem.at[1]),
    ]
    for copy in small:
        copy.start()
    for copy in small:
        copy.wait()
    blocks = [
        pltpu.make_async_copy(
            replica.at[pl.ds(pl.multiple_of(failed_s[group, i] * rows, rows), rows), :],
            block_v.at[pl.ds(i * rows, rows), :],
            block_sem.at[i],
        )
        for i in range(fails)
    ]
    for copy in blocks:
        copy.start()

    for i in range(ranks * cap):
        places_s[0, i] = -1
    for i in range(ranks):
        counts[i] = 0

    @pl.loop(0, ranks * rows)
    def _(row):
        place = dest_s[group, row]

        @pl.when(lax.div(place, rows) == me)
        def _():
            source = lax.div(row, rows)
            order = counts[source]
            places_s[0, source * cap + order] = lax.rem(place, rows)
            counts[source] = order + 1

    row_ids = lax.broadcasted_iota(jnp.int32, (rows, 128), 0)
    mask = jnp.zeros((rows, 128), jnp.float32)
    for i in range(fails):
        lost_counts[i] = 0
        for order in range(cap):
            place = places_s[0, failed_s[group, i] * cap + order]
            lost_places[i * cap + order] = place
            lost_sources[i * cap + order] = 0
            mask = jnp.where(row_ids == place, 1.0, mask)
        for r in range(rows):

            @pl.when(lax.div(dest_s[group, failed_s[group, i] * rows + r], rows) == me)
            def _(i=i, r=r):
                order = lost_counts[i]
                lost_sources[i * cap + order] = i * rows + r
                lost_counts[i] = order + 1

    lost[...] = mask
    send_places = pltpu.make_async_copy(places_s, places, small_sem.at[0])
    send_places.start()

    for copy in blocks:
        copy.wait()
    is_failed = failed_s[group, 0] == me
    sibling_failed = failed_s[group, 0] == (me ^ 1)
    for i in range(1, fails):
        is_failed = is_failed | (failed_s[group, i] == me)
        sibling_failed = sibling_failed | (failed_s[group, i] == (me ^ 1))

    @pl.when(jnp.logical_not(is_failed))
    def _():
        rows_v[...] = block_v[...].astype(jnp.float32)

    @pl.when(is_failed)
    def _():
        @pl.when(jnp.logical_not(sibling_failed))
        def _():
            copy = pltpu.make_async_copy(from_one.at[:, pl.ds(width, half)], extra_v, move_sem)
            copy.start()
            copy.wait()

        @pl.when(sibling_failed)
        def _():
            copies = [
                pltpu.make_async_copy(
                    ref.at[:, pl.ds(width, quarter)], extra_v.at[:, pl.ds(i * quarter, quarter)], move_sem
                )
                for i, ref in enumerate((from_two, from_four))
            ]
            for copy in copies:
                copy.start()
            for copy in copies:
                copy.wait()

        words = extra_v[...]
        rows_v[0:lost_rows, 0:half] = decode_short(signed_high(words))
        rows_v[0:lost_rows, half:width] = decode_short(signed_low(words))
        for j in range(lost_rows):
            lost_sources[j] = j

    def move(j):
        return pltpu.make_async_copy(
            rows_v.at[pl.ds(lost_sources[j], 1), :], base.at[pl.ds(lost_places[j], 1), :], move_sem
        )

    for j in range(lost_rows):

        @pl.when(lost_places[j] >= 0)
        def _(j=j):
            move(j).start()

    for j in range(lost_rows):

        @pl.when(lost_places[j] >= 0)
        def _(j=j):
            move(j).wait()

    send_places.wait()


def update_kernel(
    ranks, cap, elements,
    sums, lost, base, places, *refs,
):
    arrived = refs[:ranks]
    (new_master, new_first, new_second, places_s, word_one, word_two, base_v,
     master_o, first_o, second_o, small_sem, move_sem, base_sem, out_sem) = refs[ranks:]
    rows, width = word_one.shape
    chunk = width // COLUMN_CHUNKS
    me = lax.axis_index("dp")
    load_places = pltpu.make_async_copy(places, places_s, small_sem)
    load_places.start()
    load_base = pltpu.make_async_copy(base, base_v, base_sem)
    load_base.start()
    load_places.wait()

    def moves(k, order, part):
        place = places_s[0, (me ^ k) * cap + order]
        columns = pl.ds(part * chunk, chunk)
        return [
            pltpu.make_async_copy(
                arrived[k].at[pl.ds(i * cap + order, 1), columns],
                word.at[pl.ds(jnp.maximum(place, 0), 1), columns],
                move_sem.at[part],
            )
            for i, word in enumerate((word_one, word_two))
        ], place

    full = ranks * cap == rows
    for part in range(COLUMN_CHUNKS):
        for k in range(ranks):
            for order in range(cap):
                copies, place = moves(k, order, part)
                if full:
                    for copy in copies:
                        copy.start()
                else:

                    @pl.when(place >= 0)
                    def _(copies=copies):
                        for copy in copies:
                            copy.start()

    grad_total = jnp.sum(jnp.sum(sums[...], axis=0, keepdims=True), axis=1, keepdims=True)
    clip_scale = jnp.minimum(1.0, 1.0 / jnp.sqrt(grad_total / elements + clip_eps))
    is_lost = lost[:, :1] > 0.5
    load_base.wait()
    outs = []
    for part in range(COLUMN_CHUNKS):
        columns = pl.ds(part * chunk, chunk)
        for word in (word_one, word_two):
            pltpu.make_async_copy(word.at[:, columns], word.at[:, columns], move_sem.at[part]).wait()
        one, two = word_one[:, columns], word_two[:, columns]
        weights = jnp.where(is_lost, base_v[:, columns], decode_log(signed_high(one), MASTER_MAX))
        first = jnp.where(is_lost, 0.0, decode_log(signed_low(one), FIRST_MAX))
        second = jnp.where(is_lost, 0.0, decode_second(lax.shift_right_logical(two, 16)))
        grads = decode_short(signed_low(two)) * clip_scale
        first_new = beta_one * first + (1.0 - beta_one) * grads
        second_new = beta_two * second + (1.0 - beta_two) * grads * grads
        corr_one = 1.0 - beta_one**STEP
        corr_two = 1.0 - beta_two**STEP
        direction = first_new / corr_one / (jnp.sqrt(second_new / corr_two) + adam_eps) + decay_rate * weights
        master_o[:, columns] = weights - learn_rate * direction
        first_o[:, columns] = first_new
        second_o[:, columns] = second_new
        for source, target in ((master_o, new_master), (first_o, new_first), (second_o, new_second)):
            copy = pltpu.make_async_copy(source.at[:, columns], target.at[:, columns], out_sem)
            copy.start()
            outs.append(copy)
    for copy in outs:
        copy.wait()


def local(master, moment1, moment2, quant_grad, grad_exponent, replica_params, failed, dest):
    ranks = lax.axis_size("dp")
    devices = ranks * lax.axis_size("pipe")
    _, rows, width = master.shape
    fails = failed.shape[1]
    cap = (rows + ranks - 1) // ranks
    lost_rows = fails * cap
    params = pltpu.CompilerParams(vmem_limit_bytes=VMEM_LIMIT)
    i32, f32 = jnp.int32, jnp.float32
    vmem, smem, dma = pltpu.VMEM, pltpu.SMEM, pltpu.SemaphoreType.DMA

    packed = pl.pallas_call(
        functools.partial(pack_kernel, ranks, cap, fails, devices),
        out_shape=[jax.ShapeDtypeStruct((2 * cap, width + extra_columns(k, width)), i32) for k in range(ranks)]
        + [jax.ShapeDtypeStruct((devices, 128), f32)],
        in_specs=[ANY] * 8,
        out_specs=[ANY] * ranks + [pl.BlockSpec(memory_space=pltpu.VMEM)],
        scratch_shapes=[
            smem(dest.shape, i32), smem(failed.shape, i32), smem((1, rows), i32),
            smem((ranks,), i32), smem((ranks * cap,), i32),
            smem((ranks * fails,), i32), smem((ranks * lost_rows,), i32),
            vmem((rows, width), f32), vmem((rows, width), f32), vmem((rows, width), f32),
            vmem((rows, width), jnp.bfloat16),
            vmem((fails * rows, width), jnp.bfloat16), vmem((fails * rows, width), f32),
            vmem((2 * lost_rows, width), f32),
            vmem((rows, width), i32), vmem((rows, width), i32),
            vmem((2 * lost_rows, width // 2), i32),
            dma((3,)), dma((COLUMN_CHUNKS, 4)), dma((fails,)), dma, dma,
        ],
        compiler_params=params,
        name="pack",
    )(dest, failed, grad_exponent, master[0], moment1[0], moment2[0], quant_grad[0], replica_params[0, 0])
    payloads, total = packed[:ranks], packed[ranks]

    arrived = {0: payloads[0]}
    for k in [k for k in (1, 4, 2) if k < ranks] + [k for k in reversed(range(ranks)) if k not in (0, 1, 2, 4)]:
        arrived[k] = lax.ppermute(payloads[k], "dp", [(i, i ^ k) for i in range(ranks)])
    sums = lax.all_to_all(total, ("pipe", "dp"), split_axis=0, concat_axis=0, tiled=True)

    base, lost, places = pl.pallas_call(
        functools.partial(base_kernel, ranks, cap, fails),
        out_shape=[
            jax.ShapeDtypeStruct((rows, width), f32),
            jax.ShapeDtypeStruct((rows, 128), f32),
            jax.ShapeDtypeStruct((1, ranks * cap), i32),
        ],
        in_specs=[ANY] * 6,
        out_specs=[ANY, pl.BlockSpec(memory_space=pltpu.VMEM), ANY],
        scratch_shapes=[
            smem(dest.shape, i32), smem(failed.shape, i32), smem((ranks,), i32), smem((1, ranks * cap), i32),
            smem((fails,), i32), smem((lost_rows,), i32), smem((lost_rows,), i32),
            vmem((fails * rows, width), jnp.bfloat16), vmem((fails * rows, width), f32),
            vmem((lost_rows, width // 2), i32),
            dma((2,)), dma((fails,)), dma,
        ],
        compiler_params=params,
        name="base",
    )(dest, failed, replica_params[0, 0], arrived[1], arrived[2], arrived[4])

    outs = pl.pallas_call(
        functools.partial(update_kernel, ranks, cap, devices * rows * width),
        out_shape=[jax.ShapeDtypeStruct((rows, width), f32)] * 3,
        in_specs=[pl.BlockSpec(memory_space=pltpu.VMEM)] * 2 + [ANY] * (2 + ranks),
        out_specs=[ANY] * 3,
        scratch_shapes=[
            smem((1, ranks * cap), i32),
            vmem((rows, width), i32), vmem((rows, width), i32), vmem((rows, width), f32),
            vmem((rows, width), f32), vmem((rows, width), f32), vmem((rows, width), f32),
            dma, dma((COLUMN_CHUNKS,)), dma, dma,
        ],
        compiler_params=params,
        name="update",
    )(sums, lost, base, places, *[arrived[k] for k in range(ranks)])
    return tuple(out[None] for out in outs)


def solution(mesh):
    rows3 = P("pipe", "dp", None)
    in_specs = (rows3, rows3, rows3, rows3, P("pipe", "dp"), P("pipe", "dp", None, None), P(), P())
    return jax.shard_map(local, mesh=mesh, in_specs=in_specs, out_specs=(rows3,) * 3, check_vma=False)
```

time: 124 us -> 37.8 us (0.30)
  blocking collectives: 42.2 us -> 0 us
  waiting for transfers between devices: 32.3 us -> 4.58 us
  between operations: 16.9 us -> 0.74 us
  Pallas kernels: 0 us -> 14.4 us
  local copies, waits for them, and re-layouts: 15.3 us -> 2.78 us
  other arithmetic: 6.28 us -> 0 us
  starting transfers between devices: 10.5 us -> 14.9 us
    psum x1 -> x0, blocking collectives: 42.2 us -> none  [local(): grad_total = lax.psum(jnp.sum(grad * grad), ('dp', 'pipe'))]
    all_to_all x3 -> x1, waiting for transfers between devices: 20.7 us -> 2.14 us  [local(): lax.all_to_all(total, ('pipe', 'dp'), split_axis=0, concat_axis=0, tiled=...]
    pallas_call x0 -> x3, Pallas kernels: none -> 14.4 us  [the longest x1 5.57 us: local(): pl.pallas_call(functools.partial(pack_kernel, ranks, cap, fails, devices)...]
    psum x1 -> x0, waiting for transfers between devices: 11.6 us -> none  [from_root(): return lax.psum(kept, axis)]
    ppermute x0 -> x7, starting transfers between devices: none -> 8.83 us  [local(): lax.ppermute(payloads[k], 'dp', [(i, i ^ k) for i in range(ranks)])]
    gather x7 -> x0, local copies, waits for them, and re-layouts: 7.28 us -> none  [the longest x3 4.46 us: local(): values.reshape(ranks_count * peer_slots, row_width)[recv_index]]
    reshape x8 -> x0, local copies, waits for them, and re-layouts: 4.54 us -> none  [the longest x3 3.29 us: to_buffer(): return values[send_index].reshape(ranks_count, peer_slots, row_width)]
    all_to_all x3 -> x1, starting transfers between devices: 10.5 us -> 6.04 us  [local(): lax.all_to_all(total, ('pipe', 'dp'), split_axis=0, concat_axis=0, tiled=...]
  transfers between devices with their start and end apart: 4 -> 8, of which waited for: 4 -> 2; matrix products, arithmetic and copies ran while one was open for 9% -> 0% of each run, Pallas kernels for 0% -> 11%
where the time goes in v1:
time: 37.8 us; the launch traced here: 37.4 us
  starting transfers between devices  14.9 us (39%)
  Pallas kernels  14.4 us (38%)
  waiting for transfers between devices  4.58 us (12%)
  local copies, waits for them, and re-layouts  2.78 us (7%)
  between operations  0.74 us (2%)
    ppermute x7, starting transfers between devices, local(): lax.ppermute(payloads[k], 'dp', [(i, i ^ k) for i in range(ranks)])  8.83 us
    all_to_all x1, starting transfers between devices, local(): lax.all_to_all(total, ('pipe', 'dp'), split_axis=0, concat_axis=0, tiled=...  6.04 us
    pallas_call x1, Pallas kernels, local(): pl.pallas_call(functools.partial(pack_kernel, ranks, cap, fails, devices)...  5.57 us
    pallas_call x1, Pallas kernels, local(): pl.pallas_call(functools.partial(update_kernel, ranks, cap, devices * row...  4.57 us
    pallas_call x1, Pallas kernels, local(): pl.pallas_call(functools.partial(base_kernel, ranks, cap, fails), out_sha...  4.28 us
    unnamed x17, local copies, waits for them, and re-layouts  2.78 us
    ppermute x7, waiting for transfers between devices, local(): lax.ppermute(payloads[k], 'dp', [(i, i ^ k) for i in range(ranks)])  2.44 us
    all_to_all x1, waiting for transfers between devices, local(): lax.all_to_all(total, ('pipe', 'dp'), split_axis=0, concat_axis=0, tiled=...  2.14 us
  transfers between devices with their start and end apart: 8, of which 2 were waited for; matrix products, arithmetic and copies ran while one was open for 0% of the time, Pallas kernels for 11%

profile of v1, /device:TPU:0, one launch (start us, length us, event | category | flops | bytes accessed | tf_op | source)
XLA Modules:
  0.0 37.4 jit_solution(5031991444935949211)
XLA Ops:
  0.6 1.3 %copy.13.failed = s32[4,2]{1,0:T(4,128)} copy(s32[4,2]{0,1:T(2,128)} %param.14) | data formatting | bytes 64 | tf_op args[6]
  2.0 5.6 %pack.1 = (s32[4,8192]{1,0:T(4,128)}, s32[4,12288]{1,0:T(4,128)}, s32[4,10240]{1,0:T(4,128)}, s32[4,8192]{1,0:T(4,128)}, s32[4,10240]{1,0:T(4,128)}, /*index=5*/...) custom-call(s32[4,128]{1,0:T(4,128)} %dest.3, s32[4,2]{1,0:T(4,128)} %copy.13.failed, ...), custom_call_target="tpu_custom_call" | custom-call | tf_op jit(solution)/shard_map/pack/pallas_call | solution.py:435
  7.6 3.0 %collective-permute-start.1 = (s32[4,10240]{1,0:T(4,128)}, s32[4,10240]{1,0:T(4,128)S(1)}, u32[]{:S(2)}, u32[]{:S(2)}) collective-permute-start(s32[4,10240]{1,0:T(4,128)} %get-tuple-element.20), channel_id=1, source_target_pairs={{0,8},{4,12},{8,0},{12,4},{16,24},{20,28},{24,16},{28,20},{1,9},{5... | collective-permute-start | bytes 491528 | tf_op jit(solution)/shard_map/ppermute | solution.py:460
  10.6 1.5 %collective-permute-start.2 = (s32[4,10240]{1,0:T(4,128)}, s32[4,10240]{1,0:T(4,128)S(1)}, u32[]{:S(2)}, u32[]{:S(2)}) collective-permute-start(s32[4,10240]{1,0:T(4,128)} %get-tuple-element.21), channel_id=1, source_target_pairs={{0,16},{4,20},{8,24},{12,28},{16,0},{20,4},{24,8},{28,12},{1,17},{... | collective-permute-start | bytes 491528 | tf_op jit(solution)/shard_map/ppermute | solution.py:460
  12.1 0.0 collective-permute-start
  12.1 0.6 %collective-permute-start.3 = (s32[4,8192]{1,0:T(4,128)}, s32[4,8192]{1,0:T(4,128)S(1)}, u32[]{:S(2)}, u32[]{:S(2)}) collective-permute-start(s32[4,8192]{1,0:T(4,128)} %get-tuple-element.26), channel_id=1, source_target_pairs={{0,12},{4,8},{8,4},{12,0},{16,28},{20,24},{24,20},{28,16},{1,13},{... | collective-permute-start | bytes 393224 | tf_op jit(solution)/shard_map/ppermute | solution.py:460
  12.7 0.0 collective-permute-start.4
  12.7 2.4 %collective-permute-done.1.from_two.refs_2_ = s32[4,10240]{1,0:T(4,128)S(1)} collective-permute-done((s32[4,10240]{1,0:T(4,128)}, s32[4,10240]{1,0:T(4,128)S(1)}, u32[]{:S(2)}, u32[]{:S(2)}) %collective-permute-start.1) | collective-permute-done | bytes 163872 | tf_op jit(solution)/shard_map/ppermute | solution.py:460
  15.2 0.0 copy-start.1
  15.2 3.7 %collective-permute-start.5 = (s32[4,8192]{1,0:T(4,128)}, s32[4,8192]{1,0:T(4,128)S(1)}, u32[]{:S(2)}, u32[]{:S(2)}) collective-permute-start(s32[4,8192]{1,0:T(4,128)} %get-tuple-element.28), channel_id=1, source_target_pairs={{0,24},{4,28},{8,16},{12,20},{16,8},{20,12},{24,0},{28,4},{1,25},{... | collective-permute-start | bytes 393224 | tf_op jit(solution)/shard_map/ppermute | solution.py:460
  18.8 0.0 collective-permute-done.2.from_four.refs_4_
  18.8 0.0 copy-start.2
  18.8 0.0 collective-permute-start.6
  18.8 6.0 %all-to-all-start = ((f32[32,1,128]{2,1,0:T(1,128)}), f32[32,1,128]{2,1,0:T(1,128)S(1)}, u32[]{:S(2)}, u32[]{:S(2)}) async-start(f32[32,1,128]{2,1,0:T(1,128)} %bitcast.19), calls=%async_computation | async-start | bytes 32768 | tf_op jit(solution)/shard_map/all_to_all | solution.py:461
  24.9 0.0 collective-permute-done.from_one.refs_1_
  24.9 0.0 copy-done.1
  24.9 0.0 copy-done.2
  24.9 0.0 copy-start
  24.9 0.7 %copy-done = s32[4,12288]{1,0:T(4,128)} copy-done((s32[4,12288]{1,0:T(4,128)}, s32[4,12288]{1,0:T(4,128)S(1)}, u32[]{:S(2)}) %copy-start) | copy-done | bytes 196632
  25.6 4.3 %base.1 = (f32[16,8192]{1,0:T(8,128)}, f32[16,128]{1,0:T(8,128)}, s32[1,16]{1,0:T(1,128)}) custom-call(s32[4,128]{1,0:T(4,128)} %dest.3, s32[4,2]{1,0:T(4,128)} %copy.13.failed, bf16[128,8192]{1,0:T(8,128)(2,1)} %bitcast.13, s32[4,12288]{1,0:T(4,128)} %copy-done, s32[4,10240]{1,0:T(4,128)} %copy-done.1, s32[4,10240]{1,0:T(4,128)} %copy-done.2), custom_call_target="tpu_custom_call" | custom-call | tf_op jit(solution)/shard_map/base/pallas_call | solution.py:463
  29.9 2.1 %all-to-all-done = f32[32,1,128]{2,1,0:T(1,128)S(1)} async-done(((f32[32,1,128]{2,1,0:T(1,128)}), f32[32,1,128]{2,1,0:T(1,128)S(1)}, u32[]{:S(2)}, u32[]{:S(2)}) %all-to-all-start) | async-done | bytes 16416 | tf_op jit(solution)/shard_map/all_to_all | solution.py:461
  32.0 0.0 copy-start.7
  32.0 0.0 collective-permute-done.3.refs_3_
  32.0 0.0 copy-start.3
  32.0 0.0 collective-permute-done.4.refs_5_
  32.0 0.0 copy-start.4
  32.0 0.0 collective-permute-done.5.refs_6_
  32.1 0.0 copy-start.5
  32.1 0.0 collective-permute-done.6.refs_7_
  32.1 0.0 copy-start.6
  32.1 0.5 %copy-done.7 = f32[32,1,128]{2,1,0:T(1,128)} copy-done((f32[32,1,128]{2,1,0:T(1,128)}, f32[32,1,128]{2,1,0:T(1,128)S(1)}, u32[]{:S(2)}) %copy-start.7) | copy-done | bytes 16408
  32.6 0.1 copy-done.3
  32.7 0.0 copy-done.4
  32.7 0.0 copy-done.5
  32.8 0.1 copy-done.6
  32.8 4.6 %update.1 = (f32[16,8192]{1,0:T(8,128)}, f32[16,8192]{1,0:T(8,128)}, f32[16,8192]{1,0:T(8,128)}) custom-call(f32[32,128]{1,0:T(8,128)} %bitcast.18, f32[16,128]{1,0:T(8,128)} %get-tuple-element.22.lost, f32[16,8192]{1,0:T(8,128)} %get-tuple-element.23.base, s32[1,16]{1,0:T(1,128)} %get-tuple-element.24.places, s32[4,8192]{1,0:T(4,128)} %get-tuple-element.25.refs_0_, ...), custom_call_target="tpu_custom_call" | custom-call | tf_op jit(solution)/shard_map/update/pallas_call | solution.py:483
Async XLA Ops:
  7.6 7.6 %collective-permute-start.1 = (s32[4,10240]{1,0:T(4,128)}, s32[4,10240]{1,0:T(4,128)S(1)}, u32[]{:S(2)}, u32[]{:S(2)}) collective-permute-start(s32[4,10240]{1,0:T(4,128)} %get-tuple-element.20), channel_id=1, source_target_pairs={{0,8},{4,12},{8,0},{12,4},{16,24},{20,28},{24,16},{28,20},{1,9},{5... | collective-permute-start | bytes 491528 | tf_op jit(solution)/shard_map/ppermute | solution.py:460
  10.6 8.3 %collective-permute-start.2 = (s32[4,10240]{1,0:T(4,128)}, s32[4,10240]{1,0:T(4,128)S(1)}, u32[]{:S(2)}, u32[]{:S(2)}) collective-permute-start(s32[4,10240]{1,0:T(4,128)} %get-tuple-element.21), channel_id=1, source_target_pairs={{0,16},{4,20},{8,24},{12,28},{16,0},{20,4},{24,8},{28,12},{1,17},{... | collective-permute-start | bytes 491528 | tf_op jit(solution)/shard_map/ppermute | solution.py:460
  12.1 12.8 %collective-permute-start = (s32[4,12288]{1,0:T(4,128)}, s32[4,12288]{1,0:T(4,128)S(1)}, u32[]{:S(2)}, u32[]{:S(2)}) collective-permute-start(s32[4,12288]{1,0:T(4,128)} %get-tuple-element.19), channel_id=1, source_target_pairs={{0,4},{4,0},{8,12},{12,8},{16,20},{20,16},{24,28},{28,24},{1,5},{5... | collective-permute-start | bytes 589832 | tf_op jit(solution)/shard_map/ppermute | solution.py:460
  12.1 19.9 %collective-permute-start.3 = (s32[4,8192]{1,0:T(4,128)}, s32[4,8192]{1,0:T(4,128)S(1)}, u32[]{:S(2)}, u32[]{:S(2)}) collective-permute-start(s32[4,8192]{1,0:T(4,128)} %get-tuple-element.26), channel_id=1, source_target_pairs={{0,12},{4,8},{8,4},{12,0},{16,28},{20,24},{24,20},{28,16},{1,13},{... | collective-permute-start | bytes 393224 | tf_op jit(solution)/shard_map/ppermute | solution.py:460
  12.7 19.3 %collective-permute-start.4 = (s32[4,8192]{1,0:T(4,128)}, s32[4,8192]{1,0:T(4,128)S(1)}, u32[]{:S(2)}, u32[]{:S(2)}) collective-permute-start(s32[4,8192]{1,0:T(4,128)} %get-tuple-element.27), channel_id=1, source_target_pairs={{0,20},{4,16},{8,28},{12,24},{16,4},{20,0},{24,12},{28,8},{1,21},{... | collective-permute-start | bytes 393224 | tf_op jit(solution)/shard_map/ppermute | solution.py:460
  15.2 9.7 %copy-start.1 = (s32[4,10240]{1,0:T(4,128)}, s32[4,10240]{1,0:T(4,128)S(1)}, u32[]{:S(2)}) copy-start(s32[4,10240]{1,0:T(4,128)S(1)} %collective-permute-done.1.from_two.refs_2_) | copy-start | bytes 491524
  15.2 16.9 %collective-permute-start.5 = (s32[4,8192]{1,0:T(4,128)}, s32[4,8192]{1,0:T(4,128)S(1)}, u32[]{:S(2)}, u32[]{:S(2)}) collective-permute-start(s32[4,8192]{1,0:T(4,128)} %get-tuple-element.28), channel_id=1, source_target_pairs={{0,24},{4,28},{8,16},{12,20},{16,8},{20,12},{24,0},{28,4},{1,25},{... | collective-permute-start | bytes 393224 | tf_op jit(solution)/shard_map/ppermute | solution.py:460
  18.8 6.1 %copy-start.2 = (s32[4,10240]{1,0:T(4,128)}, s32[4,10240]{1,0:T(4,128)S(1)}, u32[]{:S(2)}) copy-start(s32[4,10240]{1,0:T(4,128)S(1)} %collective-permute-done.2.from_four.refs_4_) | copy-start | bytes 491524
  18.8 13.2 %collective-permute-start.6 = (s32[4,8192]{1,0:T(4,128)}, s32[4,8192]{1,0:T(4,128)S(1)}, u32[]{:S(2)}, u32[]{:S(2)}) collective-permute-start(s32[4,8192]{1,0:T(4,128)} %get-tuple-element.29), channel_id=1, source_target_pairs={{0,28},{4,24},{8,20},{12,16},{16,12},{20,8},{24,4},{28,0},{1,29},{... | collective-permute-start | bytes 393224 | tf_op jit(solution)/shard_map/ppermute | solution.py:460
  18.8 13.2 %all-to-all-start = ((f32[32,1,128]{2,1,0:T(1,128)}), f32[32,1,128]{2,1,0:T(1,128)S(1)}, u32[]{:S(2)}, u32[]{:S(2)}) async-start(f32[32,1,128]{2,1,0:T(1,128)} %bitcast.19), calls=%async_computation | async-start | bytes 32768 | tf_op jit(solution)/shard_map/all_to_all | solution.py:461
  24.9 0.7 %copy-start = (s32[4,12288]{1,0:T(4,128)}, s32[4,12288]{1,0:T(4,128)S(1)}, u32[]{:S(2)}) copy-start(s32[4,12288]{1,0:T(4,128)S(1)} %collective-permute-done.from_one.refs_1_) | copy-start | bytes 589828
  32.0 0.6 %copy-start.7 = (f32[32,1,128]{2,1,0:T(1,128)}, f32[32,1,128]{2,1,0:T(1,128)S(1)}, u32[]{:S(2)}) copy-start(f32[32,1,128]{2,1,0:T(1,128)S(1)} %all-to-all-done) | copy-start | bytes 49156
  32.0 0.7 %copy-start.3 = (s32[4,8192]{1,0:T(4,128)}, s32[4,8192]{1,0:T(4,128)S(1)}, u32[]{:S(2)}) copy-start(s32[4,8192]{1,0:T(4,128)S(1)} %collective-permute-done.3.refs_3_) | copy-start | bytes 393220
  32.0 0.7 %copy-start.4 = (s32[4,8192]{1,0:T(4,128)}, s32[4,8192]{1,0:T(4,128)S(1)}, u32[]{:S(2)}) copy-start(s32[4,8192]{1,0:T(4,128)S(1)} %collective-permute-done.4.refs_5_) | copy-start | bytes 393220
  32.1 0.7 %copy-start.5 = (s32[4,8192]{1,0:T(4,128)}, s32[4,8192]{1,0:T(4,128)S(1)}, u32[]{:S(2)}) copy-start(s32[4,8192]{1,0:T(4,128)S(1)} %collective-permute-done.5.refs_6_) | copy-start | bytes 393220
  32.1 0.7 %copy-start.6 = (s32[4,8192]{1,0:T(4,128)}, s32[4,8192]{1,0:T(4,128)S(1)}, u32[]{:S(2)}) copy-start(s32[4,8192]{1,0:T(4,128)S(1)} %collective-permute-done.6.refs_7_) | copy-start | bytes 393220

commit v2 on v1

v2 whole, which is shorter than its diff:
```python
import functools

import jax
import jax.numpy as jnp
import numpy as np
from jax import lax
from jax.experimental import pallas as pl
from jax.experimental.pallas import tpu as pltpu
from jax.sharding import PartitionSpec as P

STEP = 20

beta_one = 0.9
beta_two = 0.95
learn_rate = 0.00015
decay_rate = 0.1
adam_eps = 1e-08
clip_eps = 1e-06

MASTER_MAX = 0.1201
FIRST_MAX = 3.003
SECOND_MIN = 0.249
SECOND_MAX = 4.501

OCTAVES = 16
LOG_TOP = float(np.log(1.0 + 2.0**OCTAVES))
LOG_STEPS = 32767.0
SECOND_STEPS = 65535.0

PLACE_LANE, LOST_LANE = 0, 1
PACK_CHUNKS = 2
EXTRA_AT = 1
UPDATE_CHUNKS = 4
PACK_VMEM = 56 * 1024 * 1024
OTHER_VMEM = 8 * 1024 * 1024
ANY = pl.BlockSpec(memory_space=pl.ANY)


def with_sign(code, x):
    return jnp.where(x < 0, -code, code)


def encode_log(x, top):
    steps = jnp.log(jnp.abs(x) * (2.0**OCTAVES / top) + 1.0) * (LOG_STEPS / LOG_TOP) + 0.5
    return with_sign(steps.astype(jnp.int32), x)


def decode_log(code, top):
    size = jnp.exp(jnp.abs(code).astype(jnp.float32) * (LOG_TOP / LOG_STEPS)) * (top / 2.0**OCTAVES) - top / 2.0**OCTAVES
    return with_sign(size, code)


def encode_second(x):
    step = SECOND_STEPS / (SECOND_MAX - SECOND_MIN)
    return (x * step + (0.5 - SECOND_MIN * step)).astype(jnp.int32)


def decode_second(code):
    return code.astype(jnp.float32) * ((SECOND_MAX - SECOND_MIN) / SECOND_STEPS) + SECOND_MIN


def encode_short(x, large=False):
    size = jnp.maximum(jnp.abs(x), 2.0**-126)
    exponent = jnp.floor(jnp.log2(size) + 0.002)
    if large:
        half = jnp.floor(exponent * 0.5)
        mantissa = size * jnp.exp2(-half) * jnp.exp2(half - exponent)
    else:
        mantissa = size * jnp.exp2(-exponent)
    code = (exponent + mantissa) * 128.0 + (126.0 * 128.0 + 0.5)
    return with_sign(code.astype(jnp.int32), x)


def decode_short(code):
    size = jnp.abs(code)
    exponent = (lax.shift_right_logical(size, 7) - 127).astype(jnp.float32)
    mantissa = (size & 127).astype(jnp.float32) * (1.0 / 128.0) + 1.0
    return with_sign(mantissa * jnp.exp2(exponent), code)


def join(high, low):
    return (high << 16) | (low & 0xFFFF)


def signed_high(word):
    return word >> 16


def signed_low(word):
    return (word << 16) >> 16


def extra_columns(k, width):
    return {1: width // 2, 2: width // 4, 4: width // 4}.get(k, 0)


def pack_kernel(
    ranks, cap, fails, devices,
    dest, failed, grad_exponent, master, moment1, moment2, quant_grad, replica,
    *refs,
):
    payloads, total = refs[:ranks], refs[ranks]
    (dest_s, failed_s, exponent_s, counts, table, lost_counts, lost_table,
     master_v, first_v, second_v, grad_v, block_v, lost_v, picked_v, words, extra_v, total_v,
     small_sem, in_sem, block_sem, pick_sem, out_sem) = refs[ranks + 1:]
    rows, width = master_v.shape
    half, quarter = width // 2, width // 4
    chunk = width // PACK_CHUNKS
    lost_rows = fails * cap
    group = lax.axis_index("pipe")
    me = lax.axis_index("dp")

    small = [
        pltpu.make_async_copy(grad_exponent, exponent_s, small_sem.at[1]),
        pltpu.make_async_copy(failed, failed_s, small_sem.at[0]),
        pltpu.make_async_copy(dest, dest_s, small_sem.at[2]),
    ]
    for copy in small:
        copy.start()
    loads = []
    for part in range(PACK_CHUNKS):
        columns = pl.ds(part * chunk, chunk)
        copies = [
            pltpu.make_async_copy(source.at[:, columns], target.at[:, columns], in_sem.at[part, i])
            for i, (source, target) in enumerate(
                [(quant_grad, grad_v), (master, master_v), (moment1, first_v), (moment2, second_v)]
            )
        ]
        for copy in copies:
            copy.start()
        loads.append(copies)
    for copy in small:
        copy.wait()
    blocks = [
        pltpu.make_async_copy(
            replica.at[pl.ds(pl.multiple_of(failed_s[i, group] * rows, rows), rows), :],
            block_v.at[pl.ds(i * rows, rows), :],
            block_sem.at[i],
        )
        for i in range(fails)
    ]
    for copy in blocks:
        copy.start()

    for i in range(ranks * cap):
        table[i] = 0
    for i in range(ranks):
        counts[i] = 0
    for r in range(rows):
        target = lax.div(dest_s[group, me * rows + r], rows)
        order = counts[target]
        table[target * cap + order] = r
        counts[target] = order + 1
    for i in range(ranks * lost_rows):
        lost_table[i] = 0
    for i in range(ranks * fails):
        lost_counts[i] = 0
    for i in range(fails):
        for r in range(rows):
            target = lax.div(dest_s[group, failed_s[i, group] * rows + r], rows)
            slot = target * fails + i
            order = lost_counts[slot]
            lost_table[slot * cap + order] = i * rows + r
            lost_counts[slot] = order + 1

    row_ids = lax.broadcasted_iota(jnp.int32, (rows, 128), 0)
    exponents = jnp.zeros((rows, 128), jnp.float32)
    for r in range(rows):
        exponents = jnp.where(row_ids == r, exponent_s[0, r].astype(jnp.float32), exponents)
    row_scale = jnp.exp2(exponents)[:, :1]

    sums = jnp.zeros((8, 128), jnp.float32)
    outs, picks = [], []
    for part in range(PACK_CHUNKS):
        columns = pl.ds(part * chunk, chunk)
        if part == EXTRA_AT:
            for copy in blocks:
                copy.wait()
            lost_v[...] = block_v[...].astype(jnp.float32)
            for j in range(lost_rows):
                one, two, four = (lost_table[(me ^ k) * lost_rows + j] for k in (1, 2, 4))
                picks.append((lost_v.at[pl.ds(one, 1), :], picked_v.at[pl.ds(j, 1), :]))
                for q, source in ((0, two), (2, two), (1, four), (3, four)):
                    span = pl.ds(q * quarter, quarter)
                    picks.append((lost_v.at[pl.ds(source, 1), span], picked_v.at[pl.ds(lost_rows + j, 1), span]))
            picks = [pltpu.make_async_copy(a, b, pick_sem) for a, b in picks]
            for copy in picks:
                copy.start()
        for copy in loads[part]:
            copy.wait()
        grad = grad_v[:, columns].astype(jnp.float32) * row_scale
        sums += jnp.sum((grad * grad).reshape(rows // 8, 8, chunk // 128, 128), axis=(0, 2))
        words[0, :, columns] = join(encode_log(master_v[:, columns], MASTER_MAX), encode_log(first_v[:, columns], FIRST_MAX))
        words[1, :, columns] = join(encode_second(second_v[:, columns]), encode_short(grad))
        for k in reversed(range(ranks)):
            for order in range(cap):
                row = table[(me ^ k) * cap + order]
                copy = pltpu.make_async_copy(
                    words.at[:, pl.ds(row, 1), columns], payloads[k].at[:, pl.ds(order, 1), columns], out_sem
                )
                copy.start()
                outs.append(copy)
    total_v[...] = jnp.broadcast_to(jnp.sum(sums, axis=0, keepdims=True), (devices, 128))
    copy = pltpu.make_async_copy(total_v, total, out_sem)
    copy.start()
    outs.append(copy)

    for copy in picks:
        copy.wait()
    extra_v[...] = join(encode_short(picked_v[:, :half], True), encode_short(picked_v[:, half:], True))
    for k, first_row, first_column in ((1, 0, 0), (2, lost_rows, 0), (4, lost_rows, quarter)):
        columns = extra_columns(k, width)
        for i in range(fails):
            copy = pltpu.make_async_copy(
                extra_v.at[pl.ds(first_row + i * cap, cap), pl.ds(first_column, columns)],
                payloads[k].at[i, :, pl.ds(width, columns)],
                out_sem,
            )
            copy.start()
            outs.append(copy)
    for copy in outs:
        copy.wait()


def base_kernel(
    ranks, cap, fails,
    dest, failed, replica, from_one, from_two, from_four,
    base,
    dest_s, failed_s, counts, places_s, lost_counts, lost_sources,
    block_v, rows_v, extra_v, info_v, small_sem, block_sem, move_sem,
):
    lost_rows = fails * cap
    slots, width = base.shape[0], rows_v.shape[1]
    rows = block_v.shape[0] // fails
    half, quarter = width // 2, width // 4
    group = lax.axis_index("pipe")
    me = lax.axis_index("dp")
    small = [
        pltpu.make_async_copy(failed, failed_s, small_sem.at[0]),
        pltpu.make_async_copy(dest, dest_s, small_sem.at[1]),
    ]
    for copy in small:
        copy.start()
    for copy in small:
        copy.wait()
    blocks = [
        pltpu.make_async_copy(
            replica.at[pl.ds(pl.multiple_of(failed_s[i, group] * rows, rows), rows), :],
            block_v.at[pl.ds(i * rows, rows), :],
            block_sem.at[i],
        )
        for i in range(fails)
    ]
    for copy in blocks:
        copy.start()

    for i in range(slots):
        places_s[i] = -1
    for i in range(ranks):
        counts[i] = 0

    @pl.loop(0, ranks * rows)
    def _(row):
        place = dest_s[group, row]

        @pl.when(lax.div(place, rows) == me)
        def _():
            slot = lax.div(row, rows) ^ me
            order = counts[slot]
            places_s[slot * cap + order] = lax.rem(place, rows)
            counts[slot] = order + 1

    slot_ids = lax.broadcasted_iota(jnp.int32, (slots, 128), 0)
    places = jnp.zeros((slots, 128), jnp.int32)
    for slot in range(slots):
        places = jnp.where(slot_ids == slot, places_s[slot], places)
    source = lax.div(slot_ids, cap) ^ me
    is_lost = source == failed_s[0, group]
    for i in range(1, fails):
        is_lost = is_lost | (source == failed_s[i, group])
    lanes = lax.broadcasted_iota(jnp.int32, (slots, 128), 1)
    info_v[...] = jnp.where(lanes == PLACE_LANE, places.astype(jnp.float32), jnp.where(is_lost, 1.0, 0.0))
    send_info = pltpu.make_async_copy(info_v, base.at[:, pl.ds(width, 128)], small_sem.at[0])
    send_info.start()
    for j in range(lost_rows):
        lost_sources[j] = 0
    for i in range(fails):
        lost_counts[i] = 0
        for r in range(rows):

            @pl.when(lax.div(dest_s[group, failed_s[i, group] * rows + r], rows) == me)
            def _(i=i, r=r):
                order = lost_counts[i]
                lost_sources[i * cap + order] = i * rows + r
                lost_counts[i] = order + 1

    is_failed = failed_s[0, group] == me
    sibling_failed = failed_s[0, group] == (me ^ 1)
    for i in range(1, fails):
        is_failed = is_failed | (failed_s[i, group] == me)
        sibling_failed = sibling_failed | (failed_s[i, group] == (me ^ 1))
    for copy in blocks:
        copy.wait()

    @pl.when(jnp.logical_not(is_failed))
    def _():
        rows_v[...] = block_v[...].astype(jnp.float32)

    @pl.when(is_failed)
    def _():
        def take(source, i, first, columns):
            return pltpu.make_async_copy(
                source.at[i, :, pl.ds(width, columns)], extra_v.at[pl.ds(i * cap, cap), pl.ds(first, columns)], move_sem
            )

        @pl.when(jnp.logical_not(sibling_failed))
        def _():
            copies = [take(from_one, i, 0, half) for i in range(fails)]
            for copy in copies:
                copy.start()
            for copy in copies:
                copy.wait()

        @pl.when(sibling_failed)
        def _():
            copies = [take(ref, i, n * quarter, quarter) for i in range(fails) for n, ref in enumerate((from_two, from_four))]
            for copy in copies:
                copy.start()
            for copy in copies:
                copy.wait()

        packed = extra_v[...]
        rows_v[0:lost_rows, 0:half] = decode_short(signed_high(packed))
        rows_v[0:lost_rows, half:width] = decode_short(signed_low(packed))
        for j in range(lost_rows):
            lost_sources[j] = j

    moves = [
        pltpu.make_async_copy(
            rows_v.at[pl.ds(lost_sources[i * cap + order], 1), :],
            base.at[pl.ds((failed_s[i, group] ^ me) * cap + order, 1), pl.ds(0, width)],
            move_sem,
        )
        for i in range(fails)
        for order in range(cap)
    ]
    for copy in moves:
        copy.start()
    for copy in moves:
        copy.wait()
    send_info.wait()


def update_kernel(
    ranks, cap, elements,
    sums, base, *refs,
):
    arrived = refs[:ranks]
    (new_master, new_first, new_second, info_s, sums_v, words, base_v,
     master_o, first_o, second_o, small_sem, word_sem, out_sem) = refs[ranks:]
    rows, width = new_master.shape
    slots = base_v.shape[0]
    chunk = width // UPDATE_CHUNKS
    info = pl.ds(width, 128)
    small = [
        pltpu.make_async_copy(source, target, small_sem.at[i])
        for i, (source, target) in enumerate(
            ((sums, sums_v), (base.at[:, info], base_v.at[:, info]), (base.at[:, info], info_s))
        )
    ]
    for copy in small:
        copy.start()
    loads = []
    for part in range(UPDATE_CHUNKS):
        columns = pl.ds(part * chunk, chunk)
        copies = [pltpu.make_async_copy(base.at[:, columns], base_v.at[:, columns], word_sem.at[part])] + [
            pltpu.make_async_copy(
                arrived[k].at[:, :, columns], words.at[:, pl.ds(k * cap, cap), columns], word_sem.at[part]
            )
            for k in range(ranks)
        ]
        for copy in copies:
            copy.start()
        loads.append(copies)
    for copy in small:
        copy.wait()

    grad_total = jnp.sum(jnp.sum(sums_v[...], axis=0, keepdims=True), axis=1, keepdims=True)
    clip_scale = jnp.minimum(1.0, 1.0 / jnp.sqrt(grad_total / elements + clip_eps))
    is_lost = base_v[:, width + LOST_LANE:width + LOST_LANE + 1] > 0.5
    keep_one = jnp.where(is_lost, 0.0, beta_one)
    keep_two = jnp.where(is_lost, 0.0, beta_two)
    scale_one = 1.0 / (1.0 - beta_one**STEP)
    scale_two = 1.0 / (1.0 - beta_two**STEP)

    outs = []
    for part in range(UPDATE_CHUNKS):
        columns = pl.ds(part * chunk, chunk)
        for copy in loads[part]:
            copy.wait()
        one, two = words[0, :, columns], words[1, :, columns]
        weights = jnp.where(is_lost, base_v[:, columns], decode_log(signed_high(one), MASTER_MAX))
        first = decode_log(signed_low(one), FIRST_MAX)
        second = decode_second(lax.shift_right_logical(two, 16))
        grads = decode_short(signed_low(two)) * clip_scale
        first_new = keep_one * first + (1.0 - beta_one) * grads
        second_new = keep_two * second + (1.0 - beta_two) * grads * grads
        direction = first_new * scale_one / (jnp.sqrt(second_new * scale_two) + adam_eps) + decay_rate * weights
        master_o[:, columns] = weights - learn_rate * direction
        first_o[:, columns] = first_new
        second_o[:, columns] = second_new
        for slot in range(slots):
            place = info_s[slot, PLACE_LANE].astype(jnp.int32)

            def move(slot=slot, place=place, columns=columns):
                return [
                    pltpu.make_async_copy(a.at[pl.ds(slot, 1), columns], b.at[pl.ds(place, 1), columns], out_sem)
                    for a, b in ((master_o, new_master), (first_o, new_first), (second_o, new_second))
                ]

            if slots == rows:
                for copy in move():
                    copy.start()
            else:

                @pl.when(place >= 0)
                def _(move=move):
                    for copy in move():
                        copy.start()

    for ref in (new_master, new_first, new_second):
        pltpu.make_async_copy(ref, ref, out_sem).wait()


def local(master, moment1, moment2, quant_grad, grad_exponent, replica_params, failed, dest):
    ranks = lax.axis_size("dp")
    devices = ranks * lax.axis_size("pipe")
    _, rows, width = master.shape
    failed = failed.T
    fails = failed.shape[0]
    assert fails == 2 and ranks >= 8 and ranks & (ranks - 1) == 0
    cap = (rows + ranks - 1) // ranks
    slots = ranks * cap
    lost_rows = fails * cap
    i32, f32 = jnp.int32, jnp.float32
    vmem, smem, dma = pltpu.VMEM, pltpu.SMEM, pltpu.SemaphoreType.DMA

    packed = pl.pallas_call(
        functools.partial(pack_kernel, ranks, cap, fails, devices),
        out_shape=[jax.ShapeDtypeStruct((2, cap, width + extra_columns(k, width)), i32) for k in range(ranks)]
        + [jax.ShapeDtypeStruct((devices, 128), f32)],
        in_specs=[ANY] * 8,
        out_specs=[ANY] * (ranks + 1),
        scratch_shapes=[
            smem(dest.shape, i32), smem(failed.shape, i32), smem((1, rows), i32),
            smem((ranks,), i32), smem((slots,), i32),
            smem((ranks * fails,), i32), smem((ranks * lost_rows,), i32),
            vmem((rows, width), f32), vmem((rows, width), f32), vmem((rows, width), f32),
            vmem((rows, width), jnp.bfloat16),
            vmem((fails * rows, width), jnp.bfloat16), vmem((fails * rows, width), f32),
            vmem((2 * lost_rows, width), f32),
            vmem((2, rows, width), i32),
            vmem((2 * lost_rows, width // 2), i32), vmem((devices, 128), f32),
            dma((3,)), dma((PACK_CHUNKS, 4)), dma((fails,)), dma, dma,
        ],
        compiler_params=pltpu.CompilerParams(vmem_limit_bytes=PACK_VMEM),
        name="pack",
    )(dest, failed, grad_exponent, master[0], moment1[0], moment2[0], quant_grad[0], replica_params[0, 0])
    payloads, total = packed[:ranks], packed[ranks]

    def send(k, value):
        return lax.ppermute(value, "dp", [(i, i ^ k) for i in range(ranks)])

    arrived = {0: payloads[0], 1: send(1, payloads[1])}
    for k in [2, 4, 3, 5]:
        arrived[k] = send(k, payloads[k])
    for k in range(6, ranks):
        value, _ = lax.optimization_barrier((payloads[k], arrived[1]))
        arrived[k] = send(k, value)
    sums = lax.all_to_all(total, ("pipe", "dp"), split_axis=0, concat_axis=0, tiled=True)

    base = pl.pallas_call(
        functools.partial(base_kernel, ranks, cap, fails),
        out_shape=jax.ShapeDtypeStruct((slots, width + 128), f32),
        in_specs=[ANY] * 6,
        out_specs=ANY,
        scratch_shapes=[
            smem(dest.shape, i32), smem(failed.shape, i32), smem((ranks,), i32), smem((slots,), i32),
            smem((fails,), i32), smem((lost_rows,), i32),
            vmem((fails * rows, width), jnp.bfloat16), vmem((fails * rows, width), f32),
            vmem((lost_rows, width // 2), i32), vmem((slots, 128), f32),
            dma((2,)), dma((fails,)), dma,
        ],
        compiler_params=pltpu.CompilerParams(vmem_limit_bytes=OTHER_VMEM),
        name="base",
    )(dest, failed, replica_params[0, 0], arrived[1], arrived[2], arrived[4])

    outs = pl.pallas_call(
        functools.partial(update_kernel, ranks, cap, devices * rows * width),
        out_shape=[jax.ShapeDtypeStruct((rows, width), f32)] * 3,
        in_specs=[ANY] * (2 + ranks),
        out_specs=[ANY] * 3,
        scratch_shapes=[
            smem((slots, 128), f32), vmem((devices, 128), f32),
            vmem((2, slots, width), i32), vmem((slots, width + 128), f32),
            vmem((slots, width), f32), vmem((slots, width), f32), vmem((slots, width), f32),
            dma((3,)), dma((UPDATE_CHUNKS,)), dma,
        ],
        compiler_params=pltpu.CompilerParams(vmem_limit_bytes=OTHER_VMEM),
        name="update",
    )(sums, base, *[arrived[k] for k in range(ranks)])
    return tuple(out[None] for out in outs)


def solution(mesh):
    rows3 = P("pipe", "dp", None)
    in_specs = (rows3, rows3, rows3, rows3, P("pipe", "dp"), P("pipe", "dp", None, None), P(), P())
    return jax.shard_map(local, mesh=mesh, in_specs=in_specs, out_specs=(rows3,) * 3, check_vma=False)
```

time: 37.8 us -> 30.4 us (0.80)
  Pallas kernels: 14.4 us -> 10.3 us
  local copies, waits for them, and re-layouts: 2.78 us -> 0.02 us
  starting transfers between devices: 14.9 us -> 14.5 us
    unnamed x17 -> x8, local copies, waits for them, and re-layouts: 2.78 us -> 0.02 us
    ppermute x7, waiting for transfers between devices: 2.44 us -> 0.54 us  [send(): return lax.ppermute(value, 'dp', [(i, i ^ k) for i in range(ranks)])]
    all_to_all x1, waiting for transfers between devices: 2.14 us -> 3.97 us  [local(): lax.all_to_all(total, ('pipe', 'dp'), split_axis=0, concat_axis=0, tiled=...]
    pallas_call x1, Pallas kernels: 5.57 us -> 3.93 us  [local(): pl.pallas_call(functools.partial(pack_kernel, ranks, cap, fails, devices)...]
    pallas_call x1, Pallas kernels: 4.57 us -> 3.31 us  [local(): pl.pallas_call(functools.partial(update_kernel, ranks, cap, devices * row...]
    pallas_call x1, Pallas kernels: 4.28 us -> 3.1 us  [local(): pl.pallas_call(functools.partial(base_kernel, ranks, cap, fails), out_sha...]
    all_to_all x1, starting transfers between devices: 6.04 us -> 5 us  [local(): lax.all_to_all(total, ('pipe', 'dp'), split_axis=0, concat_axis=0, tiled=...]
    ppermute x7, starting transfers between devices: 8.83 us -> 9.53 us  [send(): return lax.ppermute(value, 'dp', [(i, i ^ k) for i in range(ranks)])]
  transfers between devices with their start and end apart: 8 -> 8, of which waited for: 2 -> 2; matrix products, arithmetic and copies ran while one was open for 0% -> 0% of each run, Pallas kernels for 11% -> 10%
where the time goes in v2:
time: 30.4 us; the launch traced here: 30.1 us
  starting transfers between devices  14.5 us (48%)
  Pallas kernels  10.3 us (34%)
  waiting for transfers between devices  4.51 us (15%)
  between operations  0.75 us (2%)
    ppermute x7, starting transfers between devices, send(): return lax.ppermute(value, 'dp', [(i, i ^ k) for i in range(ranks)])  9.53 us
    all_to_all x1, starting transfers between devices, local(): lax.all_to_all(total, ('pipe', 'dp'), split_axis=0, concat_axis=0, tiled=...  5 us
    all_to_all x1, waiting for transfers between devices, local(): lax.all_to_all(total, ('pipe', 'dp'), split_axis=0, concat_axis=0, tiled=...  3.97 us
    pallas_call x1, Pallas kernels, local(): pl.pallas_call(functools.partial(pack_kernel, ranks, cap, fails, devices)...  3.93 us
    pallas_call x1, Pallas kernels, local(): pl.pallas_call(functools.partial(update_kernel, ranks, cap, devices * row...  3.31 us
    pallas_call x1, Pallas kernels, local(): pl.pallas_call(functools.partial(base_kernel, ranks, cap, fails), out_sha...  3.1 us
  transfers between devices with their start and end apart: 8, of which 2 were waited for; matrix products, arithmetic and copies ran while one was open for 0% of the time, Pallas kernels for 10%

profile of v2, /device:TPU:0, one launch (start us, length us, event | category | flops | bytes accessed | tf_op | source)
XLA Modules:
  0.0 30.1 jit_solution(13221558564626205151)
XLA Ops:
  0.6 0.0 copy-start.2
  0.6 0.0 copy-start.3
  0.7 0.0 copy-start
  0.7 3.9 %pack.1 = (s32[2,2,8192]{2,1,0:T(2,128)}, s32[2,2,12288]{2,1,0:T(2,128)}, s32[2,2,10240]{2,1,0:T(2,128)}, s32[2,2,8192]{2,1,0:T(2,128)}, s32[2,2,10240]{2,1,0:T(...) custom-call(s32[4,128]{1,0:T(4,128)} %dest.3, ...), custom_call_target="tpu_custom_call" | custom-call | tf_op jit(solution)/shard_map/pack/pallas_call | solution.py:448
  4.6 0.0 copy-start.1
  4.6 0.5 %collective-permute-start = (s32[2,2,12288]{2,1,0:T(2,128)}, s32[2,2,12288]{2,1,0:T(2,128)S(1)}, u32[]{:S(2)}, u32[]{:S(2)}) collective-permute-start(s32[2,2,12288]{2,1,0:T(2,128)} %get-tuple-element.18), channel_id=1, source_target_pairs={{0,4},{4,0},{8,12},{12,8},{16,20},{20,16},{24,28},{28,24},{1,5},{5... | collective-permute-start | bytes 589832 | tf_op jit(solution)/shard_map/ppermute | solution.py:472
  5.1 2.6 %collective-permute-start.1 = (s32[2,2,10240]{2,1,0:T(2,128)}, s32[2,2,10240]{2,1,0:T(2,128)S(1)}, u32[]{:S(2)}, u32[]{:S(2)}) collective-permute-start(s32[2,2,10240]{2,1,0:T(2,128)} %get-tuple-element.19), channel_id=1, source_target_pairs={{0,8},{4,12},{8,0},{12,4},{16,24},{20,28},{24,16},{28,20},{1,9},{5... | collective-permute-start | bytes 491528 | tf_op jit(solution)/shard_map/ppermute | solution.py:472
  7.7 1.5 %collective-permute-start.2 = (s32[2,2,10240]{2,1,0:T(2,128)}, s32[2,2,10240]{2,1,0:T(2,128)S(1)}, u32[]{:S(2)}, u32[]{:S(2)}) collective-permute-start(s32[2,2,10240]{2,1,0:T(2,128)} %get-tuple-element.20), channel_id=1, source_target_pairs={{0,16},{4,20},{8,24},{12,28},{16,0},{20,4},{24,8},{28,12},{1,17},{... | collective-permute-start | bytes 491528 | tf_op jit(solution)/shard_map/ppermute | solution.py:472
  9.2 0.0 collective-permute-start.3
  9.2 0.3 collective-permute-start.4
  9.5 0.0 collective-permute-done.from_one.refs_1_
  9.5 2.9 %collective-permute-start.5 = (s32[2,2,8192]{2,1,0:T(2,128)}, s32[2,2,8192]{2,1,0:T(2,128)}, u32[]{:S(2)}, u32[]{:S(2)}) collective-permute-start(s32[2,2,8192]{2,1,0:T(2,128)} %get-tuple-element.25), channel_id=1, source_target_pairs={{0,24},{4,28},{8,16},{12,20},{16,8},{20,12},{24,0},{28,4},{1,25},{... | collective-permute-start | bytes 393224 | tf_op jit(solution)/shard_map/ppermute | solution.py:472
  12.4 0.5 %collective-permute-done.1.from_two.refs_2_ = s32[2,2,10240]{2,1,0:T(2,128)S(1)} collective-permute-done((s32[2,2,10240]{2,1,0:T(2,128)}, s32[2,2,10240]{2,1,0:T(2,128)S(1)}, u32[]{:S(2)}, u32[]{:S(2)}) %collective-permute-start.1) | collective-permute-done | bytes 163872 | tf_op jit(solution)/shard_map/ppermute | solution.py:472
  13.0 1.7 %collective-permute-start.6 = (s32[2,2,8192]{2,1,0:T(2,128)}, s32[2,2,8192]{2,1,0:T(2,128)}, u32[]{:S(2)}, u32[]{:S(2)}) collective-permute-start(s32[2,2,8192]{2,1,0:T(2,128)} %get-tuple-element.27), channel_id=1, source_target_pairs={{0,28},{4,24},{8,20},{12,16},{16,12},{20,8},{24,4},{28,0},{1,29},{... | collective-permute-start | bytes 393224 | tf_op jit(solution)/shard_map/ppermute | solution.py:472
  14.7 5.0 %all-to-all-start = ((f32[32,1,128]{2,1,0:T(1,128)}), f32[32,1,128]{2,1,0:T(1,128)}, u32[]{:S(2)}, u32[]{:S(2)}) async-start(f32[32,1,128]{2,1,0:T(1,128)} %bitcast.21), calls=%async_computation | async-start | bytes 32768 | tf_op jit(solution)/shard_map/all_to_all | solution.py:480
  19.7 0.0 collective-permute-done.2.from_four.refs_4_
  19.7 0.0 copy-done.2
  19.7 0.0 copy-done.3
  19.7 0.0 copy-done
  19.7 3.1 %base.1 = f32[16,8320]{1,0:T(8,128)S(1)} custom-call(s32[4,128]{1,0:T(4,128)S(1)} %copy-done.2, s32[2,4]{1,0:T(2,128)S(1)} %bitcast.16, bf16[128,8192]{1,0:T(8,128)(2,1)S(1)} %bitcast.14, s32[2,2,12288]{2,1,0:T(2,128)S(1)} %collective-permute-done.from_one.refs_1_, s32[2,2,10240]{2,1,0:T(2,128)S(1)} %collective-permute-done.1.from_two.refs_2_, ...), custom_call_target="tpu_custom_call" | custom-call | tf_op jit(solution)/shard_map/base/pallas_call | solution.py:482
  22.8 4.0 %all-to-all-done = f32[32,1,128]{2,1,0:T(1,128)} async-done(((f32[32,1,128]{2,1,0:T(1,128)}), f32[32,1,128]{2,1,0:T(1,128)}, u32[]{:S(2)}, u32[]{:S(2)}) %all-to-all-start) | async-done | bytes 16416 | tf_op jit(solution)/shard_map/all_to_all | solution.py:480
  26.8 0.0 collective-permute-done.3.refs_3_
  26.8 0.0 collective-permute-done.4.refs_5_
  26.8 0.0 collective-permute-done.5.refs_6_
  26.8 0.0 collective-permute-done.6.refs_7_
  26.8 0.0 copy-done.1
  26.8 3.3 %update.1 = (f32[16,8192]{1,0:T(8,128)}, f32[16,8192]{1,0:T(8,128)}, f32[16,8192]{1,0:T(8,128)}) custom-call(f32[32,128]{1,0:T(8,128)} %bitcast.8.sums, f32[16,8320]{1,0:T(8,128)S(1)} %base.1, s32[2,2,8192]{2,1,0:T(2,128)S(1)} %copy-done.1, s32[2,2,12288]{2,1,0:T(2,128)S(1)} %collective-permute-done.from_one.refs_1_, ...), custom_call_target="tpu_custom_call" | custom-call | tf_op jit(solution)/shard_map/update/pallas_call | solution.py:498
Async XLA Ops:
  0.6 19.1 %copy-start.2 = (s32[4,128]{1,0:T(4,128)S(1)}, s32[4,128]{1,0:T(4,128)}, u32[]{:S(2)}) copy-start(s32[4,128]{1,0:T(4,128)} %dest.3) | copy-start | bytes 6148
  0.6 19.1 %copy-start.3 = (s32[4,2]{0,1:T(2,128)S(1)}, s32[4,2]{0,1:T(2,128)}, u32[]{:S(2)}) copy-start(s32[4,2]{0,1:T(2,128)} %param.14) | copy-start | bytes 100
  0.7 19.1 %copy-start = (bf16[1,1,128,8192]{3,2,1,0:T(8,128)(2,1)S(1)}, bf16[1,1,128,8192]{3,2,1,0:T(8,128)(2,1)}, u32[]{:S(2)}) copy-start(bf16[1,1,128,8192]{3,2,1,0:T(8,128)(2,1)} %param.13) | copy-start | bytes 6291460
  4.6 22.2 %copy-start.1 = (s32[2,2,8192]{2,1,0:T(2,128)S(1)}, s32[2,2,8192]{2,1,0:T(2,128)}, u32[]{:S(2)}) copy-start(s32[2,2,8192]{2,1,0:T(2,128)} %get-tuple-element.21.refs_0_) | copy-start | bytes 393220
  4.6 4.9 %collective-permute-start = (s32[2,2,12288]{2,1,0:T(2,128)}, s32[2,2,12288]{2,1,0:T(2,128)S(1)}, u32[]{:S(2)}, u32[]{:S(2)}) collective-permute-start(s32[2,2,12288]{2,1,0:T(2,128)} %get-tuple-element.18), channel_id=1, source_target_pairs={{0,4},{4,0},{8,12},{12,8},{16,20},{20,16},{24,28},{28,24},{1,5},{5... | collective-permute-start | bytes 589832 | tf_op jit(solution)/shard_map/ppermute | solution.py:472
  5.1 7.8 %collective-permute-start.1 = (s32[2,2,10240]{2,1,0:T(2,128)}, s32[2,2,10240]{2,1,0:T(2,128)S(1)}, u32[]{:S(2)}, u32[]{:S(2)}) collective-permute-start(s32[2,2,10240]{2,1,0:T(2,128)} %get-tuple-element.19), channel_id=1, source_target_pairs={{0,8},{4,12},{8,0},{12,4},{16,24},{20,28},{24,16},{28,20},{1,9},{5... | collective-permute-start | bytes 491528 | tf_op jit(solution)/shard_map/ppermute | solution.py:472
  7.7 12.0 %collective-permute-start.2 = (s32[2,2,10240]{2,1,0:T(2,128)}, s32[2,2,10240]{2,1,0:T(2,128)S(1)}, u32[]{:S(2)}, u32[]{:S(2)}) collective-permute-start(s32[2,2,10240]{2,1,0:T(2,128)} %get-tuple-element.20), channel_id=1, source_target_pairs={{0,16},{4,20},{8,24},{12,28},{16,0},{20,4},{24,8},{28,12},{1,17},{... | collective-permute-start | bytes 491528 | tf_op jit(solution)/shard_map/ppermute | solution.py:472
  9.2 17.6 %collective-permute-start.3 = (s32[2,2,8192]{2,1,0:T(2,128)}, s32[2,2,8192]{2,1,0:T(2,128)S(1)}, u32[]{:S(2)}, u32[]{:S(2)}) collective-permute-start(s32[2,2,8192]{2,1,0:T(2,128)} %get-tuple-element.22), channel_id=1, source_target_pairs={{0,12},{4,8},{8,4},{12,0},{16,28},{20,24},{24,20},{28,16},{1,13},{... | collective-permute-start | bytes 393224 | tf_op jit(solution)/shard_map/ppermute | solution.py:472
  9.2 17.6 %collective-permute-start.4 = (s32[2,2,8192]{2,1,0:T(2,128)}, s32[2,2,8192]{2,1,0:T(2,128)S(1)}, u32[]{:S(2)}, u32[]{:S(2)}) collective-permute-start(s32[2,2,8192]{2,1,0:T(2,128)} %get-tuple-element.23), channel_id=1, source_target_pairs={{0,20},{4,16},{8,28},{12,24},{16,4},{20,0},{24,12},{28,8},{1,21},{... | collective-permute-start | bytes 393224 | tf_op jit(solution)/shard_map/ppermute | solution.py:472
  9.5 17.3 %collective-permute-start.5 = (s32[2,2,8192]{2,1,0:T(2,128)}, s32[2,2,8192]{2,1,0:T(2,128)}, u32[]{:S(2)}, u32[]{:S(2)}) collective-permute-start(s32[2,2,8192]{2,1,0:T(2,128)} %get-tuple-element.25), channel_id=1, source_target_pairs={{0,24},{4,28},{8,16},{12,20},{16,8},{20,12},{24,0},{28,4},{1,25},{... | collective-permute-start | bytes 393224 | tf_op jit(solution)/shard_map/ppermute | solution.py:472
  13.0 13.9 %collective-permute-start.6 = (s32[2,2,8192]{2,1,0:T(2,128)}, s32[2,2,8192]{2,1,0:T(2,128)}, u32[]{:S(2)}, u32[]{:S(2)}) collective-permute-start(s32[2,2,8192]{2,1,0:T(2,128)} %get-tuple-element.27), channel_id=1, source_target_pairs={{0,28},{4,24},{8,20},{12,16},{16,12},{20,8},{24,4},{28,0},{1,29},{... | collective-permute-start | bytes 393224 | tf_op jit(solution)/shard_map/ppermute | solution.py:472
  14.7 12.1 %all-to-all-start = ((f32[32,1,128]{2,1,0:T(1,128)}), f32[32,1,128]{2,1,0:T(1,128)}, u32[]{:S(2)}, u32[]{:S(2)}) async-start(f32[32,1,128]{2,1,0:T(1,128)} %bitcast.21), calls=%async_computation | async-start | bytes 32768 | tf_op jit(solution)/shard_map/all_to_all | solution.py:480

commit v3 on v2

--- a/solution.py
+++ b/solution.py
@@ -90,8 +90,14 @@
     return (word << 16) >> 16
 
 
-def extra_columns(k, width):
-    return {1: width // 2, 2: width // 4, 4: width // 4}.get(k, 0)
+def payload_shape(k, cap, width):
+    if k < 2:
+        return (2, cap, width + k * (width // 2))
+    return (2, 2, cap, width + (width // 8 if k in (2, 4) else 0))
+
+
+def sent_kinds(ranks):
+    return [0, 1] + list(range(2, ranks, 2))
 
 
 def pack_kernel(
@@ -99,12 +105,13 @@
     dest, failed, grad_exponent, master, moment1, moment2, quant_grad, replica,
     *refs,
 ):
-    payloads, total = refs[:ranks], refs[ranks]
+    kinds = sent_kinds(ranks)
+    payloads, total = dict(zip(kinds, refs)), refs[len(kinds)]
     (dest_s, failed_s, exponent_s, counts, table, lost_counts, lost_table,
      master_v, first_v, second_v, grad_v, block_v, lost_v, picked_v, words, extra_v, total_v,
-     small_sem, in_sem, block_sem, pick_sem, out_sem) = refs[ranks + 1:]
+     small_sem, in_sem, block_sem, pick_sem, out_sem) = refs[len(kinds) + 1:]
     rows, width = master_v.shape
-    half, quarter = width // 2, width // 4
+    half, quarter, eighth = width // 2, width // 4, width // 8
     chunk = width // PACK_CHUNKS
     lost_rows = fails * cap
     group = lax.axis_index("pipe")
@@ -195,8 +202,9 @@
         for k in reversed(range(ranks)):
             for order in range(cap):
                 row = table[(me ^ k) * cap + order]
+                target = payloads[k] if k < 2 else payloads[k - k % 2].at[k % 2]
                 copy = pltpu.make_async_copy(
-                    words.at[:, pl.ds(row, 1), columns], payloads[k].at[:, pl.ds(order, 1), columns], out_sem
+                    words.at[:, pl.ds(row, 1), columns], target.at[:, pl.ds(order, 1), columns], out_sem
                 )
                 copy.start()
                 outs.append(copy)
@@ -208,12 +216,16 @@
     for copy in picks:
         copy.wait()
     extra_v[...] = join(encode_short(picked_v[:, :half], True), encode_short(picked_v[:, half:], True))
-    for k, first_row, first_column in ((1, 0, 0), (2, lost_rows, 0), (4, lost_rows, quarter)):
-        columns = extra_columns(k, width)
+    extras = [(payloads[1], 0, 0, half)] + [
+        (payloads[k].at[part], lost_rows, first + part * eighth, eighth)
+        for k, first in ((2, 0), (4, quarter))
+        for part in range(2)
+    ]
+    for target, first_row, first_column, columns in extras:
         for i in range(fails):
             copy = pltpu.make_async_copy(
                 extra_v.at[pl.ds(first_row + i * cap, cap), pl.ds(first_column, columns)],
-                payloads[k].at[i, :, pl.ds(width, columns)],
+                target.at[i, :, pl.ds(width, columns)],
                 out_sem,
             )
             copy.start()
@@ -226,18 +238,19 @@
     ranks, cap, fails,
     dest, failed, replica, from_one, from_two, from_four,
     base,
-    dest_s, failed_s, counts, places_s, lost_counts, lost_sources,
+    dest_s, failed_s, dest_v, lost_counts, lost_sources,
     block_v, rows_v, extra_v, info_v, small_sem, block_sem, move_sem,
 ):
     lost_rows = fails * cap
     slots, width = base.shape[0], rows_v.shape[1]
     rows = block_v.shape[0] // fails
-    half, quarter = width // 2, width // 4
+    half, eighth = width // 2, width // 8
     group = lax.axis_index("pipe")
     me = lax.axis_index("dp")
     small = [
         pltpu.make_async_copy(failed, failed_s, small_sem.at[0]),
         pltpu.make_async_copy(dest, dest_s, small_sem.at[1]),
+        pltpu.make_async_copy(dest, dest_v, small_sem.at[2]),
     ]
     for copy in small:
         copy.start()
@@ -254,32 +267,27 @@
     for copy in blocks:
         copy.start()
 
-    for i in range(slots):
-        places_s[i] = -1
-    for i in range(ranks):
-        counts[i] = 0
-
-    @pl.loop(0, ranks * rows)
-    def _(row):
-        place = dest_s[group, row]
-
-        @pl.when(lax.div(place, rows) == me)
-        def _():
-            slot = lax.div(row, rows) ^ me
-            order = counts[slot]
-            places_s[slot * cap + order] = lax.rem(place, rows)
-            counts[slot] = order + 1
-
+    every = ranks * rows
+    row_ids = lax.broadcasted_iota(jnp.int32, (every, every), 0)
+    column_ids = lax.broadcasted_iota(jnp.int32, (every, every), 1)
+    place = dest_v[pl.ds(group, 1), :]
+    mine = jnp.where(lax.div(place, rows) == me, 1.0, 0.0)
+    mine_down = jnp.sum(jnp.where(row_ids == column_ids, mine, 0.0), axis=1, keepdims=True)
+    earlier = (row_ids < column_ids) & (lax.div(row_ids, rows) == lax.div(column_ids, rows))
+    order = jnp.sum(jnp.where(earlier, mine_down, 0.0), axis=0, keepdims=True).astype(jnp.int32)
+    columns = lax.broadcasted_iota(jnp.int32, (1, every), 1)
+    slot_of = jnp.where(mine > 0.5, (lax.div(columns, rows) ^ me) * cap + order, -1)
+    slot_rows = lax.broadcasted_iota(jnp.int32, (slots, every), 0)
+    found = slot_rows == slot_of
+    place_in = lax.rem(place, rows).astype(jnp.float32)
+    places = jnp.sum(jnp.where(found, place_in + 1.0, 0.0), axis=1, keepdims=True) - 1.0
     slot_ids = lax.broadcasted_iota(jnp.int32, (slots, 128), 0)
-    places = jnp.zeros((slots, 128), jnp.int32)
-    for slot in range(slots):
-        places = jnp.where(slot_ids == slot, places_s[slot], places)
     source = lax.div(slot_ids, cap) ^ me
     is_lost = source == failed_s[0, group]
     for i in range(1, fails):
         is_lost = is_lost | (source == failed_s[i, group])
     lanes = lax.broadcasted_iota(jnp.int32, (slots, 128), 1)
-    info_v[...] = jnp.where(lanes == PLACE_LANE, places.astype(jnp.float32), jnp.where(is_lost, 1.0, 0.0))
+    info_v[...] = jnp.where(lanes == PLACE_LANE, places, jnp.where(is_lost, 1.0, 0.0))
     send_info = pltpu.make_async_copy(info_v, base.at[:, pl.ds(width, 128)], small_sem.at[0])
     send_info.start()
     for j in range(lost_rows):
@@ -323,7 +331,8 @@
 
         @pl.when(sibling_failed)
         def _():
-            copies = [take(ref, i, n * quarter, quarter) for i in range(fails) for n, ref in enumerate((from_two, from_four))]
+            parts = (from_two.at[0], from_two.at[1], from_four.at[0], from_four.at[1])
+            copies = [take(ref, i, n * eighth, eighth) for i in range(fails) for n, ref in enumerate(parts)]
             for copy in copies:
                 copy.start()
             for copy in copies:
@@ -355,7 +364,10 @@
     ranks, cap, elements,
     sums, base, *refs,
 ):
-    arrived = refs[:ranks]
+    kinds = sent_kinds(ranks)
+    arrived = dict(zip(kinds, refs))
+    for k, ref in zip(range(2, ranks, 2), refs[len(kinds):ranks]):
+        arrived[k], arrived[k + 1] = arrived[k].at[0], ref.at[1]
     (new_master, new_first, new_second, info_s, sums_v, words, base_v,
      master_o, first_o, second_o, small_sem, word_sem, out_sem) = refs[ranks:]
     rows, width = new_master.shape
@@ -441,16 +453,17 @@
     assert fails == 2 and ranks >= 8 and ranks & (ranks - 1) == 0
     cap = (rows + ranks - 1) // ranks
     slots = ranks * cap
+    kinds = sent_kinds(ranks)
     lost_rows = fails * cap
     i32, f32 = jnp.int32, jnp.float32
     vmem, smem, dma = pltpu.VMEM, pltpu.SMEM, pltpu.SemaphoreType.DMA
 
     packed = pl.pallas_call(
         functools.partial(pack_kernel, ranks, cap, fails, devices),
-        out_shape=[jax.ShapeDtypeStruct((2, cap, width + extra_columns(k, width)), i32) for k in range(ranks)]
+        out_shape=[jax.ShapeDtypeStruct(payload_shape(k, cap, width), i32) for k in kinds]
         + [jax.ShapeDtypeStruct((devices, 128), f32)],
         in_specs=[ANY] * 8,
-        out_specs=[ANY] * (ranks + 1),
+        out_specs=[ANY] * (len(kinds) + 1),
         scratch_shapes=[
             smem(dest.shape, i32), smem(failed.shape, i32), smem((1, rows), i32),
             smem((ranks,), i32), smem((slots,), i32),
@@ -466,18 +479,22 @@
         compiler_params=pltpu.CompilerParams(vmem_limit_bytes=PACK_VMEM),
         name="pack",
     )(dest, failed, grad_exponent, master[0], moment1[0], moment2[0], quant_grad[0], replica_params[0, 0])
-    payloads, total = packed[:ranks], packed[ranks]
+    payloads, total = dict(zip(kinds, packed)), packed[-1]
 
     def send(k, value):
         return lax.ppermute(value, "dp", [(i, i ^ k) for i in range(ranks)])
 
     arrived = {0: payloads[0], 1: send(1, payloads[1])}
-    for k in [2, 4, 3, 5]:
-        arrived[k] = send(k, payloads[k])
-    for k in range(6, ranks):
-        value, _ = lax.optimization_barrier((payloads[k], arrived[1]))
+    for k in range(2, ranks, 2):
+        value = payloads[k]
+        if k not in (2, 4):
+            value, _ = lax.optimization_barrier((value, arrived[1]))
         arrived[k] = send(k, value)
     sums = lax.all_to_all(total, ("pipe", "dp"), split_axis=0, concat_axis=0, tiled=True)
+    handed = []
+    for k in range(2, ranks, 2):
+        value, _ = lax.optimization_barrier((arrived[k], sums))
+        handed.append(send(1, value))
 
     base = pl.pallas_call(
         functools.partial(base_kernel, ranks, cap, fails),
@@ -485,11 +502,11 @@
         in_specs=[ANY] * 6,
         out_specs=ANY,
         scratch_shapes=[
-            smem(dest.shape, i32), smem(failed.shape, i32), smem((ranks,), i32), smem((slots,), i32),
+            smem(dest.shape, i32), smem(failed.shape, i32), vmem(dest.shape, i32),
             smem((fails,), i32), smem((lost_rows,), i32),
             vmem((fails * rows, width), jnp.bfloat16), vmem((fails * rows, width), f32),
             vmem((lost_rows, width // 2), i32), vmem((slots, 128), f32),
-            dma((2,)), dma((fails,)), dma,
+            dma((3,)), dma((fails,)), dma,
         ],
         compiler_params=pltpu.CompilerParams(vmem_limit_bytes=OTHER_VMEM),
         name="base",
@@ -508,7 +525,7 @@
         ],
         compiler_params=pltpu.CompilerParams(vmem_limit_bytes=OTHER_VMEM),
         name="update",
-    )(sums, base, *[arrived[k] for k in range(ranks)])
+    )(sums, base, *[arrived[k] for k in kinds], *handed)
     return tuple(out[None] for out in outs)
 
 

time: 30.4 us -> 28.6 us (0.941)
  blocking collectives: 0 us -> 12.6 us
  starting transfers between devices: 14.5 us -> 6.19 us
  waiting for transfers between devices: 4.51 us -> 0.6 us
  Pallas kernels: 10.3 us -> 8.3 us
    all_to_all x0 -> x1, blocking collectives: none -> 12.6 us  [local(): lax.all_to_all(total, ('pipe', 'dp'), split_axis=0, concat_axis=0, tiled=...]
    all_to_all x1 -> x0, starting transfers between devices: 5 us -> none  [local(): lax.all_to_all(total, ('pipe', 'dp'), split_axis=0, concat_axis=0, tiled=...]
    all_to_all x1 -> x0, waiting for transfers between devices: 3.97 us -> none  [local(): lax.all_to_all(total, ('pipe', 'dp'), split_axis=0, concat_axis=0, tiled=...]
    ppermute x7, starting transfers between devices: 9.53 us -> 6.19 us  [send(): return lax.ppermute(value, 'dp', [(i, i ^ k) for i in range(ranks)])]
    pallas_call x1, Pallas kernels: 3.1 us -> 1.17 us  [local(): pl.pallas_call(functools.partial(base_kernel, ranks, cap, fails), out_sha...]
  transfers between devices with their start and end apart: 8 -> 7, of which waited for: 2 -> 2; matrix products, arithmetic and copies ran while one was open for 0% -> 0% of each run, Pallas kernels for 10% -> 4%
where the time goes in v3:
time: 28.6 us; the launch traced here: 28.4 us
  blocking collectives  12.6 us (44%)
  Pallas kernels  8.3 us (29%)
  starting transfers between devices  6.19 us (22%)
  between operations  0.7 us (2%)
  waiting for transfers between devices  0.6 us (2%)
    all_to_all x1, blocking collectives, local(): lax.all_to_all(total, ('pipe', 'dp'), split_axis=0, concat_axis=0, tiled=...  12.6 us
    ppermute x7, starting transfers between devices, send(): return lax.ppermute(value, 'dp', [(i, i ^ k) for i in range(ranks)])  6.19 us
    pallas_call x1, Pallas kernels, local(): pl.pallas_call(functools.partial(pack_kernel, ranks, cap, fails, devices)...  3.93 us
    pallas_call x1, Pallas kernels, local(): pl.pallas_call(functools.partial(update_kernel, ranks, cap, devices * row...  3.2 us
    pallas_call x1, Pallas kernels, local(): pl.pallas_call(functools.partial(base_kernel, ranks, cap, fails), out_sha...  1.17 us
    ppermute x7, waiting for transfers between devices, send(): return lax.ppermute(value, 'dp', [(i, i ^ k) for i in range(ranks)])  0.6 us
  transfers between devices with their start and end apart: 7, of which 2 were waited for; matrix products, arithmetic and copies ran while one was open for 0% of the time, Pallas kernels for 4%

profile of v3, /device:TPU:0, one launch (start us, length us, event | category | flops | bytes accessed | tf_op | source)
XLA Modules:
  0.0 28.4 jit_solution(2789321997582772564)
XLA Ops:
  0.6 0.0 copy-start.2
  0.6 0.0 copy-start.3
  0.7 0.0 copy-start
  0.7 3.9 %pack.1 = (s32[2,2,8192]{2,1,0:T(2,128)}, s32[2,2,12288]{2,1,0:T(2,128)}, s32[2,2,2,9216]{3,2,1,0:T(2,128)}, s32[2,2,2,9216]{3,2,1,0:T(2,128)}, s32[2,2,2,8192]{3,2,1,0:T(2,128)}, /*index=5*/f32[32,128]{1,0:T(8,128)}) custom-call(s32[4,128]{1,0:T(4,128)} %dest.3, s32[2,4]{1,0:T(2,128)} %bitcast.16, s32[1,16]{1,0:T(1,128)} %grad_exponent.1, ...), custom_call_target="tpu_custom_call" | custom-call | tf_op jit(solution)/shard_map/pack/pallas_call | solution.py:461
  4.6 0.0 copy-start.1
  4.6 0.5 %collective-permute-start = (s32[2,2,12288]{2,1,0:T(2,128)}, s32[2,2,12288]{2,1,0:T(2,128)S(1)}, u32[]{:S(2)}, u32[]{:S(2)}) collective-permute-start(s32[2,2,12288]{2,1,0:T(2,128)} %get-tuple-element.17), channel_id=1, source_target_pairs={{0,4},{4,0},{8,12},{12,8},{16,20},{20,16},{24,28},{28,24},{1,5},{5... | collective-permute-start | bytes 589832 | tf_op jit(solution)/shard_map/ppermute | solution.py:485
  5.1 2.6 %collective-permute-start.1 = (s32[2,2,2,9216]{3,2,1,0:T(2,128)}, s32[2,2,2,9216]{3,2,1,0:T(2,128)S(1)}, u32[]{:S(2)}, u32[]{:S(2)}) collective-permute-start(s32[2,2,2,9216]{3,2,1,0:T(2,128)} %get-tuple-element.18), channel_id=1, source_target_pairs={{0,8},{4,12},{8,0},{12,4},{16,24},{20,28},{24,16},{28,20},{1,9},{5... | collective-permute-start | bytes 884744 | tf_op jit(solution)/shard_map/ppermute | solution.py:485
  7.7 1.5 %collective-permute-start.2 = (s32[2,2,2,9216]{3,2,1,0:T(2,128)}, s32[2,2,2,9216]{3,2,1,0:T(2,128)S(1)}, u32[]{:S(2)}, u32[]{:S(2)}) collective-permute-start(s32[2,2,2,9216]{3,2,1,0:T(2,128)} %get-tuple-element.19), channel_id=1, source_target_pairs={{0,16},{4,20},{8,24},{12,28},{16,0},{20,4},{24,8},{28,12},{1,17},{... | collective-permute-start | bytes 884744 | tf_op jit(solution)/shard_map/ppermute | solution.py:485
  9.2 0.0 collective-permute-done.from_one.refs_1_
  9.2 1.0 %collective-permute-start.3 = (s32[2,2,2,8192]{3,2,1,0:T(2,128)}, s32[2,2,2,8192]{3,2,1,0:T(2,128)S(1)}, u32[]{:S(2)}, u32[]{:S(2)}) collective-permute-start(s32[2,2,2,8192]{3,2,1,0:T(2,128)} %get-tuple-element.22), channel_id=1, source_target_pairs={{0,24},{4,28},{8,16},{12,20},{16,8},{20,12},{24,0},{28,4},{1,25},{... | collective-permute-start | bytes 786440 | tf_op jit(solution)/shard_map/ppermute | solution.py:485
  10.2 12.6 %all_to_all.11 = f32[32,1,128]{2,1,0:T(1,128)S(1)} all-to-all(f32[32,1,128]{2,1,0:T(1,128)} %bitcast.22), channel_id=1, replica_groups=mesh['dp'=8,'pipe'=4] {'pipe','dp'}, dimensions={0} | all-to-all | bytes 32768 | tf_op jit(solution)/shard_map/all_to_all | solution.py:493
  22.8 0.0 collective-permute-done.1.from_two.refs_2_
  22.8 0.0 collective-permute-start.4
  22.9 0.0 collective-permute-done.2.from_four.refs_3_
  22.9 0.5 %collective-permute-start.5 = (s32[2,2,2,9216]{3,2,1,0:T(2,128)S(1)}, s32[2,2,2,9216]{3,2,1,0:T(2,128)S(1)}, u32[]{:S(2)}, u32[]{:S(2)}) collective-permute-start(s32[2,2,2,9216]{3,2,1,0:T(2,128)S(1)} %collective-permute-done.2.from_four.refs_3_), channel_id=1, source_target_pairs={{0,4},{4,0},{8,12},{12,8},{16,20},{20,16},{24,28},{28,24},{1,5},{5... | collective-permute-start | bytes 884744 | tf_op jit(solution)/shard_map/ppermute | solution.py:485
  23.3 0.0 collective-permute-done.3.refs_4_
  23.4 0.1 collective-permute-start.6
  23.4 0.0 copy-done.2
  23.4 0.0 copy-done.3
  23.4 0.0 copy-done
  23.4 1.2 %base.1 = f32[16,8320]{1,0:T(8,128)S(1)} custom-call(s32[4,128]{1,0:T(4,128)S(1)} %copy-done.2, s32[2,4]{1,0:T(2,128)S(1)} %bitcast.17, bf16[128,8192]{1,0:T(8,128)(2,1)S(1)} %bitcast.14, s32[2,2,12288]{2,1,0:T(2,128)S(1)} %collective-permute-done.from_one.refs_1_, s32[2,2,2,9216]{3,2,1,0:T(2,128)S(1)} %collective-permute-done.1.from_two.refs_2_, ...), custom_call_target="tpu_custom_call" | custom-call | tf_op jit(solution)/shard_map/base/pallas_call | solution.py:499
  24.6 0.0 collective-permute-done.4.refs_5_
  24.6 0.2 collective-permute-done.5.refs_6_
  24.8 0.4 %collective-permute-done.6.refs_7_ = s32[2,2,2,8192]{3,2,1,0:T(2,128)S(1)} collective-permute-done((s32[2,2,2,8192]{3,2,1,0:T(2,128)S(1)}, s32[2,2,2,8192]{3,2,1,0:T(2,128)S(1)}, u32[]{:S(2)}, u32[]{:S(2)}) %collective-permute-start.6) | collective-permute-done | bytes 262176 | tf_op jit(solution)/shard_map/ppermute | solution.py:485
  25.2 0.0 copy-done.1
  25.2 3.2 %update.1 = (f32[16,8192]{1,0:T(8,128)}, f32[16,8192]{1,0:T(8,128)}, f32[16,8192]{1,0:T(8,128)}) custom-call(f32[32,128]{1,0:T(8,128)S(1)} %bitcast.15, f32[16,8320]{1,0:T(8,128)S(1)} %base.1, s32[2,2,8192]{2,1,0:T(2,128)S(1)} %copy-done.1, s32[2,2,12288]{2,1,0:T(2,128)S(1)} %collective-permute-done.from_one.refs_1_, ...), custom_call_target="tpu_custom_call" | custom-call | tf_op jit(solution)/shard_map/update/pallas_call | solution.py:515
Async XLA Ops:
  0.6 22.8 %copy-start.2 = (s32[4,128]{1,0:T(4,128)S(1)}, s32[4,128]{1,0:T(4,128)}, u32[]{:S(2)}) copy-start(s32[4,128]{1,0:T(4,128)} %dest.3) | copy-start | bytes 6148
  0.6 22.8 %copy-start.3 = (s32[4,2]{0,1:T(2,128)S(1)}, s32[4,2]{0,1:T(2,128)}, u32[]{:S(2)}) copy-start(s32[4,2]{0,1:T(2,128)} %param.14) | copy-start | bytes 100
  0.7 22.8 %copy-start = (bf16[1,1,128,8192]{3,2,1,0:T(8,128)(2,1)S(1)}, bf16[1,1,128,8192]{3,2,1,0:T(8,128)(2,1)}, u32[]{:S(2)}) copy-start(bf16[1,1,128,8192]{3,2,1,0:T(8,128)(2,1)} %param.13) | copy-start | bytes 6291460
  4.6 20.6 %copy-start.1 = (s32[2,2,8192]{2,1,0:T(2,128)S(1)}, s32[2,2,8192]{2,1,0:T(2,128)}, u32[]{:S(2)}) copy-start(s32[2,2,8192]{2,1,0:T(2,128)} %get-tuple-element.20.refs_0_) | copy-start | bytes 393220
  4.6 4.6 %collective-permute-start = (s32[2,2,12288]{2,1,0:T(2,128)}, s32[2,2,12288]{2,1,0:T(2,128)S(1)}, u32[]{:S(2)}, u32[]{:S(2)}) collective-permute-start(s32[2,2,12288]{2,1,0:T(2,128)} %get-tuple-element.17), channel_id=1, source_target_pairs={{0,4},{4,0},{8,12},{12,8},{16,20},{20,16},{24,28},{28,24},{1,5},{5... | collective-permute-start | bytes 589832 | tf_op jit(solution)/shard_map/ppermute | solution.py:485
  5.1 17.7 %collective-permute-start.1 = (s32[2,2,2,9216]{3,2,1,0:T(2,128)}, s32[2,2,2,9216]{3,2,1,0:T(2,128)S(1)}, u32[]{:S(2)}, u32[]{:S(2)}) collective-permute-start(s32[2,2,2,9216]{3,2,1,0:T(2,128)} %get-tuple-element.18), channel_id=1, source_target_pairs={{0,8},{4,12},{8,0},{12,4},{16,24},{20,28},{24,16},{28,20},{1,9},{5... | collective-permute-start | bytes 884744 | tf_op jit(solution)/shard_map/ppermute | solution.py:485
  7.7 15.2 %collective-permute-start.2 = (s32[2,2,2,9216]{3,2,1,0:T(2,128)}, s32[2,2,2,9216]{3,2,1,0:T(2,128)S(1)}, u32[]{:S(2)}, u32[]{:S(2)}) collective-permute-start(s32[2,2,2,9216]{3,2,1,0:T(2,128)} %get-tuple-element.19), channel_id=1, source_target_pairs={{0,16},{4,20},{8,24},{12,28},{16,0},{20,4},{24,8},{28,12},{1,17},{... | collective-permute-start | bytes 884744 | tf_op jit(solution)/shard_map/ppermute | solution.py:485
  9.2 14.1 %collective-permute-start.3 = (s32[2,2,2,8192]{3,2,1,0:T(2,128)}, s32[2,2,2,8192]{3,2,1,0:T(2,128)S(1)}, u32[]{:S(2)}, u32[]{:S(2)}) collective-permute-start(s32[2,2,2,8192]{3,2,1,0:T(2,128)} %get-tuple-element.22), channel_id=1, source_target_pairs={{0,24},{4,28},{8,16},{12,20},{16,8},{20,12},{24,0},{28,4},{1,25},{... | collective-permute-start | bytes 786440 | tf_op jit(solution)/shard_map/ppermute | solution.py:485
  22.8 1.8 %collective-permute-start.4 = (s32[2,2,2,9216]{3,2,1,0:T(2,128)S(1)}, s32[2,2,2,9216]{3,2,1,0:T(2,128)S(1)}, u32[]{:S(2)}, u32[]{:S(2)}) collective-permute-start(s32[2,2,2,9216]{3,2,1,0:T(2,128)S(1)} %collective-permute-done.1.from_two.refs_2_), channel_id=1, source_target_pairs={{0,4},{4,0},{8,12},{12,8},{16,20},{20,16},{24,28},{28,24},{1,5},{5... | collective-permute-start | bytes 884744 | tf_op jit(solution)/shard_map/ppermute | solution.py:485
  22.9 2.0 %collective-permute-start.5 = (s32[2,2,2,9216]{3,2,1,0:T(2,128)S(1)}, s32[2,2,2,9216]{3,2,1,0:T(2,128)S(1)}, u32[]{:S(2)}, u32[]{:S(2)}) collective-permute-start(s32[2,2,2,9216]{3,2,1,0:T(2,128)S(1)} %collective-permute-done.2.from_four.refs_3_), channel_id=1, source_target_pairs={{0,4},{4,0},{8,12},{12,8},{16,20},{20,16},{24,28},{28,24},{1,5},{5... | collective-permute-start | bytes 884744 | tf_op jit(solution)/shard_map/ppermute | solution.py:485
  23.4 1.9 %collective-permute-start.6 = (s32[2,2,2,8192]{3,2,1,0:T(2,128)S(1)}, s32[2,2,2,8192]{3,2,1,0:T(2,128)S(1)}, u32[]{:S(2)}, u32[]{:S(2)}) collective-permute-start(s32[2,2,2,8192]{3,2,1,0:T(2,128)S(1)} %collective-permute-done.3.refs_4_), channel_id=1, source_target_pairs={{0,4},{4,0},{8,12},{12,8},{16,20},{20,16},{24,28},{28,24},{1,5},{5... | collective-permute-start | bytes 786440 | tf_op jit(solution)/shard_map/ppermute | solution.py:485

commit v4 on v3

--- a/solution.py
+++ b/solution.py
@@ -25,14 +25,15 @@
 OCTAVES = 16
 LOG_TOP = float(np.log(1.0 + 2.0**OCTAVES))
 LOG_STEPS = 32767.0
+LN_TWO = float(np.log(2.0))
 SECOND_STEPS = 65535.0
 
 PLACE_LANE, LOST_LANE = 0, 1
 PACK_CHUNKS = 2
 EXTRA_AT = 1
-UPDATE_CHUNKS = 4
+UPDATE_CHUNKS = 2
 PACK_VMEM = 56 * 1024 * 1024
-OTHER_VMEM = 8 * 1024 * 1024
+OTHER_VMEM = 12 * 1024 * 1024
 ANY = pl.BlockSpec(memory_space=pl.ANY)
 
 
@@ -46,7 +47,7 @@
 
 
 def decode_log(code, top):
-    size = jnp.exp(jnp.abs(code).astype(jnp.float32) * (LOG_TOP / LOG_STEPS)) * (top / 2.0**OCTAVES) - top / 2.0**OCTAVES
+    size = jnp.exp2(jnp.abs(code).astype(jnp.float32) * (LOG_TOP / LOG_STEPS / LN_TWO)) * (top / 2.0**OCTAVES) - top / 2.0**OCTAVES
     return with_sign(size, code)
 
 
@@ -61,7 +62,7 @@
 
 def encode_short(x, large=False):
     size = jnp.maximum(jnp.abs(x), 2.0**-126)
-    exponent = jnp.floor(jnp.log2(size) + 0.002)
+    exponent = jnp.floor(jnp.log(size) * (1.0 / LN_TWO) + 0.002)
     if large:
         half = jnp.floor(exponent * 0.5)
         mantissa = size * jnp.exp2(-half) * jnp.exp2(half - exponent)
@@ -170,6 +171,14 @@
             lost_table[slot * cap + order] = i * rows + r
             lost_counts[slot] = order + 1
 
+    def has_failed(rank):
+        found = failed_s[0, group] == rank
+        for i in range(1, fails):
+            found = found | (failed_s[i, group] == rank)
+        return found
+
+    helped = jnp.where(has_failed(me ^ 1), me ^ 1, jnp.where(has_failed(me ^ 2) & has_failed(me ^ 3), me ^ 2, me ^ 4))
+
     row_ids = lax.broadcasted_iota(jnp.int32, (rows, 128), 0)
     exponents = jnp.zeros((rows, 128), jnp.float32)
     for r in range(rows):
@@ -177,7 +186,7 @@
     row_scale = jnp.exp2(exponents)[:, :1]
 
     sums = jnp.zeros((8, 128), jnp.float32)
-    outs, picks = [], []
+    picks = []
     for part in range(PACK_CHUNKS):
         columns = pl.ds(part * chunk, chunk)
         if part == EXTRA_AT:
@@ -185,12 +194,8 @@
                 copy.wait()
             lost_v[...] = block_v[...].astype(jnp.float32)
             for j in range(lost_rows):
-                one, two, four = (lost_table[(me ^ k) * lost_rows + j] for k in (1, 2, 4))
-                picks.append((lost_v.at[pl.ds(one, 1), :], picked_v.at[pl.ds(j, 1), :]))
-                for q, source in ((0, two), (2, two), (1, four), (3, four)):
-                    span = pl.ds(q * quarter, quarter)
-                    picks.append((lost_v.at[pl.ds(source, 1), span], picked_v.at[pl.ds(lost_rows + j, 1), span]))
-            picks = [pltpu.make_async_copy(a, b, pick_sem) for a, b in picks]
+                source = lost_table[helped * lost_rows + j]
+                picks.append(pltpu.make_async_copy(lost_v.at[pl.ds(source, 1), :], picked_v.at[pl.ds(j, 1), :], pick_sem))
             for copy in picks:
                 copy.start()
         for copy in loads[part]:
@@ -207,31 +212,27 @@
                     words.at[:, pl.ds(row, 1), columns], target.at[:, pl.ds(order, 1), columns], out_sem
                 )
                 copy.start()
-                outs.append(copy)
     total_v[...] = jnp.broadcast_to(jnp.sum(sums, axis=0, keepdims=True), (devices, 128))
-    copy = pltpu.make_async_copy(total_v, total, out_sem)
-    copy.start()
-    outs.append(copy)
+    pltpu.make_async_copy(total_v, total, out_sem).start()
 
     for copy in picks:
         copy.wait()
     extra_v[...] = join(encode_short(picked_v[:, :half], True), encode_short(picked_v[:, half:], True))
-    extras = [(payloads[1], 0, 0, half)] + [
-        (payloads[k].at[part], lost_rows, first + part * eighth, eighth)
+    extras = [(payloads[1], 0, half)] + [
+        (payloads[k].at[part], first + part * eighth, eighth)
         for k, first in ((2, 0), (4, quarter))
         for part in range(2)
     ]
-    for target, first_row, first_column, columns in extras:
+    for target, first_column, columns in extras:
         for i in range(fails):
             copy = pltpu.make_async_copy(
-                extra_v.at[pl.ds(first_row + i * cap, cap), pl.ds(first_column, columns)],
+                extra_v.at[pl.ds(i * cap, cap), pl.ds(first_column, columns)],
                 target.at[i, :, pl.ds(width, columns)],
                 out_sem,
             )
             copy.start()
-            outs.append(copy)
-    for copy in outs:
-        copy.wait()
+    for ref in refs[:len(kinds) + 1]:
+        pltpu.make_async_copy(ref, ref, out_sem).wait()
 
 
 def base_kernel(
@@ -382,7 +383,6 @@
     ]
     for copy in small:
         copy.start()
-    loads = []
     for part in range(UPDATE_CHUNKS):
         columns = pl.ds(part * chunk, chunk)
         copies = [pltpu.make_async_copy(base.at[:, columns], base_v.at[:, columns], word_sem.at[part])] + [
@@ -393,7 +393,6 @@
         ]
         for copy in copies:
             copy.start()
-        loads.append(copies)
     for copy in small:
         copy.wait()
 
@@ -405,11 +404,10 @@
     scale_one = 1.0 / (1.0 - beta_one**STEP)
     scale_two = 1.0 / (1.0 - beta_two**STEP)
 
-    outs = []
     for part in range(UPDATE_CHUNKS):
         columns = pl.ds(part * chunk, chunk)
-        for copy in loads[part]:
-            copy.wait()
+        for ref in (words.at[:, :, columns], base_v.at[:, columns]):
+            pltpu.make_async_copy(ref, ref, word_sem.at[part]).wait()
         one, two = words[0, :, columns], words[1, :, columns]
         weights = jnp.where(is_lost, base_v[:, columns], decode_log(signed_high(one), MASTER_MAX))
         first = decode_log(signed_low(one), FIRST_MAX)
@@ -417,8 +415,10 @@
         grads = decode_short(signed_low(two)) * clip_scale
         first_new = keep_one * first + (1.0 - beta_one) * grads
         second_new = keep_two * second + (1.0 - beta_two) * grads * grads
-        direction = first_new * scale_one / (jnp.sqrt(second_new * scale_two) + adam_eps) + decay_rate * weights
-        master_o[:, columns] = weights - learn_rate * direction
+        spread = second_new * scale_two
+        root = spread * lax.rsqrt(jnp.maximum(spread, 1e-37))
+        step = first_new * (learn_rate * scale_one) / (root + adam_eps)
+        master_o[:, columns] = weights * (1.0 - learn_rate * decay_rate) - step
         first_o[:, columns] = first_new
         second_o[:, columns] = second_new
         for slot in range(slots):
@@ -471,9 +471,9 @@
             vmem((rows, width), f32), vmem((rows, width), f32), vmem((rows, width), f32),
             vmem((rows, width), jnp.bfloat16),
             vmem((fails * rows, width), jnp.bfloat16), vmem((fails * rows, width), f32),
-            vmem((2 * lost_rows, width), f32),
+            vmem((lost_rows, width), f32),
             vmem((2, rows, width), i32),
-            vmem((2 * lost_rows, width // 2), i32), vmem((devices, 128), f32),
+            vmem((lost_rows, width // 2), i32), vmem((devices, 128), f32),
             dma((3,)), dma((PACK_CHUNKS, 4)), dma((fails,)), dma, dma,
         ],
         compiler_params=pltpu.CompilerParams(vmem_limit_bytes=PACK_VMEM),

time: 28.6 us -> 28.2 us (0.986)
  Pallas kernels: 8.3 us -> 7.93 us
where the time goes in v4:
time: 28.2 us; the launch traced here: 28 us
  blocking collectives  12.6 us (45%)
  Pallas kernels  7.93 us (28%)
  starting transfers between devices  6.19 us (22%)
  between operations  0.7 us (2%)
  waiting for transfers between devices  0.6 us (2%)
    all_to_all x1, blocking collectives, local(): lax.all_to_all(total, ('pipe', 'dp'), split_axis=0, concat_axis=0, tiled=...  12.6 us
    ppermute x7, starting transfers between devices, send(): return lax.ppermute(value, 'dp', [(i, i ^ k) for i in range(ranks)])  6.19 us
    pallas_call x1, Pallas kernels, local(): pl.pallas_call(functools.partial(pack_kernel, ranks, cap, fails, devices)...  3.74 us
    pallas_call x1, Pallas kernels, local(): pl.pallas_call(functools.partial(update_kernel, ranks, cap, devices * row...  3.02 us
    pallas_call x1, Pallas kernels, local(): pl.pallas_call(functools.partial(base_kernel, ranks, cap, fails), out_sha...  1.17 us
    ppermute x7, waiting for transfers between devices, send(): return lax.ppermute(value, 'dp', [(i, i ^ k) for i in range(ranks)])  0.6 us
  transfers between devices with their start and end apart: 7, of which 2 were waited for; matrix products, arithmetic and copies ran while one was open for 0% of the time, Pallas kernels for 4%

profile of v4, /device:TPU:0, one launch (start us, length us, event | category | flops | bytes accessed | tf_op | source)
XLA Modules:
  0.0 28.0 jit_solution(13907120004666817169)
XLA Ops:
  0.6 0.0 copy-start.2
  0.6 0.0 copy-start.3
  0.7 0.0 copy-start
  0.7 3.7 %pack.1 = (s32[2,2,8192]{2,1,0:T(2,128)}, s32[2,2,12288]{2,1,0:T(2,128)}, s32[2,2,2,9216]{3,2,1,0:T(2,128)}, s32[2,2,2,9216]{3,2,1,0:T(2,128)}, s32[2,2,2,8192]{3,2,1,0:T(2,128)}, /*index=5*/f32[32,128]{1,0:T(8,128)}) custom-call(s32[4,128]{1,0:T(4,128)} %dest.3, s32[2,4]{1,0:T(2,128)} %bitcast.16, s32[1,16]{1,0:T(1,128)} %grad_exponent.1, ...), custom_call_target="tpu_custom_call" | custom-call | tf_op jit(solution)/shard_map/pack/pallas_call | solution.py:461
  4.4 0.0 copy-start.1
  4.4 0.5 %collective-permute-start = (s32[2,2,12288]{2,1,0:T(2,128)}, s32[2,2,12288]{2,1,0:T(2,128)S(1)}, u32[]{:S(2)}, u32[]{:S(2)}) collective-permute-start(s32[2,2,12288]{2,1,0:T(2,128)} %get-tuple-element.17), channel_id=1, source_target_pairs={{0,4},{4,0},{8,12},{12,8},{16,20},{20,16},{24,28},{28,24},{1,5},{5... | collective-permute-start | bytes 589832 | tf_op jit(solution)/shard_map/ppermute | solution.py:485
  4.9 2.6 %collective-permute-start.1 = (s32[2,2,2,9216]{3,2,1,0:T(2,128)}, s32[2,2,2,9216]{3,2,1,0:T(2,128)S(1)}, u32[]{:S(2)}, u32[]{:S(2)}) collective-permute-start(s32[2,2,2,9216]{3,2,1,0:T(2,128)} %get-tuple-element.18), channel_id=1, source_target_pairs={{0,8},{4,12},{8,0},{12,4},{16,24},{20,28},{24,16},{28,20},{1,9},{5... | collective-permute-start | bytes 884744 | tf_op jit(solution)/shard_map/ppermute | solution.py:485
  7.5 1.5 %collective-permute-start.2 = (s32[2,2,2,9216]{3,2,1,0:T(2,128)}, s32[2,2,2,9216]{3,2,1,0:T(2,128)S(1)}, u32[]{:S(2)}, u32[]{:S(2)}) collective-permute-start(s32[2,2,2,9216]{3,2,1,0:T(2,128)} %get-tuple-element.19), channel_id=1, source_target_pairs={{0,16},{4,20},{8,24},{12,28},{16,0},{20,4},{24,8},{28,12},{1,17},{... | collective-permute-start | bytes 884744 | tf_op jit(solution)/shard_map/ppermute | solution.py:485
  9.0 0.0 collective-permute-done.from_one.refs_1_
  9.0 1.0 %collective-permute-start.3 = (s32[2,2,2,8192]{3,2,1,0:T(2,128)}, s32[2,2,2,8192]{3,2,1,0:T(2,128)S(1)}, u32[]{:S(2)}, u32[]{:S(2)}) collective-permute-start(s32[2,2,2,8192]{3,2,1,0:T(2,128)} %get-tuple-element.22), channel_id=1, source_target_pairs={{0,24},{4,28},{8,16},{12,20},{16,8},{20,12},{24,0},{28,4},{1,25},{... | collective-permute-start | bytes 786440 | tf_op jit(solution)/shard_map/ppermute | solution.py:485
  10.0 12.6 %all_to_all.11 = f32[32,1,128]{2,1,0:T(1,128)S(1)} all-to-all(f32[32,1,128]{2,1,0:T(1,128)} %bitcast.22), channel_id=1, replica_groups=mesh['dp'=8,'pipe'=4] {'pipe','dp'}, dimensions={0} | all-to-all | bytes 32768 | tf_op jit(solution)/shard_map/all_to_all | solution.py:493
  22.6 0.0 collective-permute-done.1.from_two.refs_2_
  22.6 0.0 collective-permute-start.4
  22.7 0.0 collective-permute-done.2.from_four.refs_3_
  22.7 0.5 %collective-permute-start.5 = (s32[2,2,2,9216]{3,2,1,0:T(2,128)S(1)}, s32[2,2,2,9216]{3,2,1,0:T(2,128)S(1)}, u32[]{:S(2)}, u32[]{:S(2)}) collective-permute-start(s32[2,2,2,9216]{3,2,1,0:T(2,128)S(1)} %collective-permute-done.2.from_four.refs_3_), channel_id=1, source_target_pairs={{0,4},{4,0},{8,12},{12,8},{16,20},{20,16},{24,28},{28,24},{1,5},{5... | collective-permute-start | bytes 884744 | tf_op jit(solution)/shard_map/ppermute | solution.py:485
  23.2 0.0 collective-permute-done.3.refs_4_
  23.2 0.1 collective-permute-start.6
  23.2 0.0 copy-done.2
  23.2 0.0 copy-done.3
  23.2 0.0 copy-done
  23.2 1.2 %base.1 = f32[16,8320]{1,0:T(8,128)S(1)} custom-call(s32[4,128]{1,0:T(4,128)S(1)} %copy-done.2, s32[2,4]{1,0:T(2,128)S(1)} %bitcast.17, bf16[128,8192]{1,0:T(8,128)(2,1)S(1)} %bitcast.14, s32[2,2,12288]{2,1,0:T(2,128)S(1)} %collective-permute-done.from_one.refs_1_, s32[2,2,2,9216]{3,2,1,0:T(2,128)S(1)} %collective-permute-done.1.from_two.refs_2_, ...), custom_call_target="tpu_custom_call" | custom-call | tf_op jit(solution)/shard_map/base/pallas_call | solution.py:499
  24.4 0.0 collective-permute-done.4.refs_5_
  24.4 0.2 collective-permute-done.5.refs_6_
  24.6 0.4 %collective-permute-done.6.refs_7_ = s32[2,2,2,8192]{3,2,1,0:T(2,128)S(1)} collective-permute-done((s32[2,2,2,8192]{3,2,1,0:T(2,128)S(1)}, s32[2,2,2,8192]{3,2,1,0:T(2,128)S(1)}, u32[]{:S(2)}, u32[]{:S(2)}) %collective-permute-start.6) | collective-permute-done | bytes 262176 | tf_op jit(solution)/shard_map/ppermute | solution.py:485
  25.0 0.0 copy-done.1
  25.0 3.0 %update.1 = (f32[16,8192]{1,0:T(8,128)}, f32[16,8192]{1,0:T(8,128)}, f32[16,8192]{1,0:T(8,128)}) custom-call(f32[32,128]{1,0:T(8,128)S(1)} %bitcast.15, f32[16,8320]{1,0:T(8,128)S(1)} %base.1, s32[2,2,8192]{2,1,0:T(2,128)S(1)} %copy-done.1, s32[2,2,12288]{2,1,0:T(2,128)S(1)} %collective-permute-done.from_one.refs_1_, ...), custom_call_target="tpu_custom_call" | custom-call | tf_op jit(solution)/shard_map/update/pallas_call | solution.py:515
Async XLA Ops:
  0.6 22.6 %copy-start.2 = (s32[4,128]{1,0:T(4,128)S(1)}, s32[4,128]{1,0:T(4,128)}, u32[]{:S(2)}) copy-start(s32[4,128]{1,0:T(4,128)} %dest.3) | copy-start | bytes 6148
  0.6 22.6 %copy-start.3 = (s32[4,2]{0,1:T(2,128)S(1)}, s32[4,2]{0,1:T(2,128)}, u32[]{:S(2)}) copy-start(s32[4,2]{0,1:T(2,128)} %param.14) | copy-start | bytes 100
  0.7 22.6 %copy-start = (bf16[1,1,128,8192]{3,2,1,0:T(8,128)(2,1)S(1)}, bf16[1,1,128,8192]{3,2,1,0:T(8,128)(2,1)}, u32[]{:S(2)}) copy-start(bf16[1,1,128,8192]{3,2,1,0:T(8,128)(2,1)} %param.13) | copy-start | bytes 6291460
  4.4 20.6 %copy-start.1 = (s32[2,2,8192]{2,1,0:T(2,128)S(1)}, s32[2,2,8192]{2,1,0:T(2,128)}, u32[]{:S(2)}) copy-start(s32[2,2,8192]{2,1,0:T(2,128)} %get-tuple-element.20.refs_0_) | copy-start | bytes 393220
  4.4 4.6 %collective-permute-start = (s32[2,2,12288]{2,1,0:T(2,128)}, s32[2,2,12288]{2,1,0:T(2,128)S(1)}, u32[]{:S(2)}, u32[]{:S(2)}) collective-permute-start(s32[2,2,12288]{2,1,0:T(2,128)} %get-tuple-element.17), channel_id=1, source_target_pairs={{0,4},{4,0},{8,12},{12,8},{16,20},{20,16},{24,28},{28,24},{1,5},{5... | collective-permute-start | bytes 589832 | tf_op jit(solution)/shard_map/ppermute | solution.py:485
  4.9 17.7 %collective-permute-start.1 = (s32[2,2,2,9216]{3,2,1,0:T(2,128)}, s32[2,2,2,9216]{3,2,1,0:T(2,128)S(1)}, u32[]{:S(2)}, u32[]{:S(2)}) collective-permute-start(s32[2,2,2,9216]{3,2,1,0:T(2,128)} %get-tuple-element.18), channel_id=1, source_target_pairs={{0,8},{4,12},{8,0},{12,4},{16,24},{20,28},{24,16},{28,20},{1,9},{5... | collective-permute-start | bytes 884744 | tf_op jit(solution)/shard_map/ppermute | solution.py:485
  7.5 15.2 %collective-permute-start.2 = (s32[2,2,2,9216]{3,2,1,0:T(2,128)}, s32[2,2,2,9216]{3,2,1,0:T(2,128)S(1)}, u32[]{:S(2)}, u32[]{:S(2)}) collective-permute-start(s32[2,2,2,9216]{3,2,1,0:T(2,128)} %get-tuple-element.19), channel_id=1, source_target_pairs={{0,16},{4,20},{8,24},{12,28},{16,0},{20,4},{24,8},{28,12},{1,17},{... | collective-permute-start | bytes 884744 | tf_op jit(solution)/shard_map/ppermute | solution.py:485
  9.0 14.1 %collective-permute-start.3 = (s32[2,2,2,8192]{3,2,1,0:T(2,128)}, s32[2,2,2,8192]{3,2,1,0:T(2,128)S(1)}, u32[]{:S(2)}, u32[]{:S(2)}) collective-permute-start(s32[2,2,2,8192]{3,2,1,0:T(2,128)} %get-tuple-element.22), channel_id=1, source_target_pairs={{0,24},{4,28},{8,16},{12,20},{16,8},{20,12},{24,0},{28,4},{1,25},{... | collective-permute-start | bytes 786440 | tf_op jit(solution)/shard_map/ppermute | solution.py:485
  22.6 1.8 %collective-permute-start.4 = (s32[2,2,2,9216]{3,2,1,0:T(2,128)S(1)}, s32[2,2,2,9216]{3,2,1,0:T(2,128)S(1)}, u32[]{:S(2)}, u32[]{:S(2)}) collective-permute-start(s32[2,2,2,9216]{3,2,1,0:T(2,128)S(1)} %collective-permute-done.1.from_two.refs_2_), channel_id=1, source_target_pairs={{0,4},{4,0},{8,12},{12,8},{16,20},{20,16},{24,28},{28,24},{1,5},{5... | collective-permute-start | bytes 884744 | tf_op jit(solution)/shard_map/ppermute | solution.py:485
  22.7 2.0 %collective-permute-start.5 = (s32[2,2,2,9216]{3,2,1,0:T(2,128)S(1)}, s32[2,2,2,9216]{3,2,1,0:T(2,128)S(1)}, u32[]{:S(2)}, u32[]{:S(2)}) collective-permute-start(s32[2,2,2,9216]{3,2,1,0:T(2,128)S(1)} %collective-permute-done.2.from_four.refs_3_), channel_id=1, source_target_pairs={{0,4},{4,0},{8,12},{12,8},{16,20},{20,16},{24,28},{28,24},{1,5},{5... | collective-permute-start | bytes 884744 | tf_op jit(solution)/shard_map/ppermute | solution.py:485
  23.2 1.9 %collective-permute-start.6 = (s32[2,2,2,8192]{3,2,1,0:T(2,128)S(1)}, s32[2,2,2,8192]{3,2,1,0:T(2,128)S(1)}, u32[]{:S(2)}, u32[]{:S(2)}) collective-permute-start(s32[2,2,2,8192]{3,2,1,0:T(2,128)S(1)} %collective-permute-done.3.refs_4_), channel_id=1, source_target_pairs={{0,4},{4,0},{8,12},{12,8},{16,20},{20,16},{24,28},{28,24},{1,5},{5... | collective-permute-start | bytes 786440 | tf_op jit(solution)/shard_map/ppermute | solution.py:485

commit v5 on v4

--- a/solution.py
+++ b/solution.py
@@ -29,12 +29,17 @@
 SECOND_STEPS = 65535.0
 
 PLACE_LANE, LOST_LANE = 0, 1
-PACK_CHUNKS = 2
+PACK_PARTS = (5, 3)
 EXTRA_AT = 1
-UPDATE_CHUNKS = 2
+UPDATE_PARTS = (3, 5)
 PACK_VMEM = 56 * 1024 * 1024
 OTHER_VMEM = 12 * 1024 * 1024
 ANY = pl.BlockSpec(memory_space=pl.ANY)
+
+
+def spans(width, parts):
+    ends = np.cumsum(parts) * width // sum(parts)
+    return [pl.ds(int(end) - part * width // sum(parts), part * width // sum(parts)) for part, end in zip(parts, ends)]
 
 
 def with_sign(code, x):
@@ -113,7 +118,6 @@
      small_sem, in_sem, block_sem, pick_sem, out_sem) = refs[len(kinds) + 1:]
     rows, width = master_v.shape
     half, quarter, eighth = width // 2, width // 4, width // 8
-    chunk = width // PACK_CHUNKS
     lost_rows = fails * cap
     group = lax.axis_index("pipe")
     me = lax.axis_index("dp")
@@ -126,8 +130,7 @@
     for copy in small:
         copy.start()
     loads = []
-    for part in range(PACK_CHUNKS):
-        columns = pl.ds(part * chunk, chunk)
+    for part, columns in enumerate(spans(width, PACK_PARTS)):
         copies = [
             pltpu.make_async_copy(source.at[:, columns], target.at[:, columns], in_sem.at[part, i])
             for i, (source, target) in enumerate(
@@ -187,8 +190,7 @@
 
     sums = jnp.zeros((8, 128), jnp.float32)
     picks = []
-    for part in range(PACK_CHUNKS):
-        columns = pl.ds(part * chunk, chunk)
+    for part, columns in enumerate(spans(width, PACK_PARTS)):
         if part == EXTRA_AT:
             for copy in blocks:
                 copy.wait()
@@ -201,7 +203,7 @@
         for copy in loads[part]:
             copy.wait()
         grad = grad_v[:, columns].astype(jnp.float32) * row_scale
-        sums += jnp.sum((grad * grad).reshape(rows // 8, 8, chunk // 128, 128), axis=(0, 2))
+        sums += jnp.sum((grad * grad).reshape(rows // 8, 8, -1, 128), axis=(0, 2))
         words[0, :, columns] = join(encode_log(master_v[:, columns], MASTER_MAX), encode_log(first_v[:, columns], FIRST_MAX))
         words[1, :, columns] = join(encode_second(second_v[:, columns]), encode_short(grad))
         for k in reversed(range(ranks)):
@@ -373,7 +375,6 @@
      master_o, first_o, second_o, small_sem, word_sem, out_sem) = refs[ranks:]
     rows, width = new_master.shape
     slots = base_v.shape[0]
-    chunk = width // UPDATE_CHUNKS
     info = pl.ds(width, 128)
     small = [
         pltpu.make_async_copy(source, target, small_sem.at[i])
@@ -383,8 +384,7 @@
     ]
     for copy in small:
         copy.start()
-    for part in range(UPDATE_CHUNKS):
-        columns = pl.ds(part * chunk, chunk)
+    for part, columns in enumerate(spans(width, UPDATE_PARTS)):
         copies = [pltpu.make_async_copy(base.at[:, columns], base_v.at[:, columns], word_sem.at[part])] + [
             pltpu.make_async_copy(
                 arrived[k].at[:, :, columns], words.at[:, pl.ds(k * cap, cap), columns], word_sem.at[part]
@@ -404,8 +404,7 @@
     scale_one = 1.0 / (1.0 - beta_one**STEP)
     scale_two = 1.0 / (1.0 - beta_two**STEP)
 
-    for part in range(UPDATE_CHUNKS):
-        columns = pl.ds(part * chunk, chunk)
+    for part, columns in enumerate(spans(width, UPDATE_PARTS)):
         for ref in (words.at[:, :, columns], base_v.at[:, columns]):
             pltpu.make_async_copy(ref, ref, word_sem.at[part]).wait()
         one, two = words[0, :, columns], words[1, :, columns]
@@ -474,7 +473,7 @@
             vmem((lost_rows, width), f32),
             vmem((2, rows, width), i32),
             vmem((lost_rows, width // 2), i32), vmem((devices, 128), f32),
-            dma((3,)), dma((PACK_CHUNKS, 4)), dma((fails,)), dma, dma,
+            dma((3,)), dma((len(PACK_PARTS), 4)), dma((fails,)), dma, dma,
         ],
         compiler_params=pltpu.CompilerParams(vmem_limit_bytes=PACK_VMEM),
         name="pack",
@@ -521,7 +520,7 @@
             smem((slots, 128), f32), vmem((devices, 128), f32),
             vmem((2, slots, width), i32), vmem((slots, width + 128), f32),
             vmem((slots, width), f32), vmem((slots, width), f32), vmem((slots, width), f32),
-            dma((3,)), dma((UPDATE_CHUNKS,)), dma,
+            dma((3,)), dma((len(UPDATE_PARTS),)), dma,
         ],
         compiler_params=pltpu.CompilerParams(vmem_limit_bytes=OTHER_VMEM),
         name="update",

time: 28.2 us -> 28.1 us (level)
  no operation moved by 1% of the time
where the time goes in v5:
time: 28.1 us; the launch traced here: 28 us
  blocking collectives  12.6 us (45%)
  Pallas kernels  7.84 us (28%)
  starting transfers between devices  6.19 us (22%)
  between operations  0.7 us (2%)
  waiting for transfers between devices  0.6 us (2%)
    all_to_all x1, blocking collectives, local(): lax.all_to_all(total, ('pipe', 'dp'), split_axis=0, concat_axis=0, tiled=...  12.6 us
    ppermute x7, starting transfers between devices, send(): return lax.ppermute(value, 'dp', [(i, i ^ k) for i in range(ranks)])  6.19 us
    pallas_call x1, Pallas kernels, local(): pl.pallas_call(functools.partial(pack_kernel, ranks, cap, fails, devices)...  3.74 us
    pallas_call x1, Pallas kernels, local(): pl.pallas_call(functools.partial(update_kernel, ranks, cap, devices * row...  2.93 us
    pallas_call x1, Pallas kernels, local(): pl.pallas_call(functools.partial(base_kernel, ranks, cap, fails), out_sha...  1.17 us
    ppermute x7, waiting for transfers between devices, send(): return lax.ppermute(value, 'dp', [(i, i ^ k) for i in range(ranks)])  0.6 us
  transfers between devices with their start and end apart: 7, of which 2 were waited for; matrix products, arithmetic and copies ran while one was open for 0% of the time, Pallas kernels for 4%

profile of v5, /device:TPU:0, one launch (start us, length us, event | category | flops | bytes accessed | tf_op | source)
XLA Modules:
  0.0 28.0 jit_solution(3381094716786275590)
XLA Ops:
  0.6 0.0 copy-start.2
  0.6 0.0 copy-start.3
  0.7 0.0 copy-start
  0.7 3.7 %pack.1 = (s32[2,2,8192]{2,1,0:T(2,128)}, s32[2,2,12288]{2,1,0:T(2,128)}, s32[2,2,2,9216]{3,2,1,0:T(2,128)}, s32[2,2,2,9216]{3,2,1,0:T(2,128)}, s32[2,2,2,8192]{3,2,1,0:T(2,128)}, /*index=5*/f32[32,128]{1,0:T(8,128)}) custom-call(s32[4,128]{1,0:T(4,128)} %dest.3, s32[2,4]{1,0:T(2,128)} %bitcast.16, s32[1,16]{1,0:T(1,128)} %grad_exponent.1, ...), custom_call_target="tpu_custom_call" | custom-call | tf_op jit(solution)/shard_map/pack/pallas_call | solution.py:460
  4.4 0.0 copy-start.1
  4.4 0.5 %collective-permute-start = (s32[2,2,12288]{2,1,0:T(2,128)}, s32[2,2,12288]{2,1,0:T(2,128)S(1)}, u32[]{:S(2)}, u32[]{:S(2)}) collective-permute-start(s32[2,2,12288]{2,1,0:T(2,128)} %get-tuple-element.17), channel_id=1, source_target_pairs={{0,4},{4,0},{8,12},{12,8},{16,20},{20,16},{24,28},{28,24},{1,5},{5... | collective-permute-start | bytes 589832 | tf_op jit(solution)/shard_map/ppermute | solution.py:484
  4.9 2.6 %collective-permute-start.1 = (s32[2,2,2,9216]{3,2,1,0:T(2,128)}, s32[2,2,2,9216]{3,2,1,0:T(2,128)S(1)}, u32[]{:S(2)}, u32[]{:S(2)}) collective-permute-start(s32[2,2,2,9216]{3,2,1,0:T(2,128)} %get-tuple-element.18), channel_id=1, source_target_pairs={{0,8},{4,12},{8,0},{12,4},{16,24},{20,28},{24,16},{28,20},{1,9},{5... | collective-permute-start | bytes 884744 | tf_op jit(solution)/shard_map/ppermute | solution.py:484
  7.5 1.5 %collective-permute-start.2 = (s32[2,2,2,9216]{3,2,1,0:T(2,128)}, s32[2,2,2,9216]{3,2,1,0:T(2,128)S(1)}, u32[]{:S(2)}, u32[]{:S(2)}) collective-permute-start(s32[2,2,2,9216]{3,2,1,0:T(2,128)} %get-tuple-element.19), channel_id=1, source_target_pairs={{0,16},{4,20},{8,24},{12,28},{16,0},{20,4},{24,8},{28,12},{1,17},{... | collective-permute-start | bytes 884744 | tf_op jit(solution)/shard_map/ppermute | solution.py:484
  9.0 0.0 collective-permute-done.from_one.refs_1_
  9.0 1.0 %collective-permute-start.3 = (s32[2,2,2,8192]{3,2,1,0:T(2,128)}, s32[2,2,2,8192]{3,2,1,0:T(2,128)S(1)}, u32[]{:S(2)}, u32[]{:S(2)}) collective-permute-start(s32[2,2,2,8192]{3,2,1,0:T(2,128)} %get-tuple-element.22), channel_id=1, source_target_pairs={{0,24},{4,28},{8,16},{12,20},{16,8},{20,12},{24,0},{28,4},{1,25},{... | collective-permute-start | bytes 786440 | tf_op jit(solution)/shard_map/ppermute | solution.py:484
  10.0 12.6 %all_to_all.11 = f32[32,1,128]{2,1,0:T(1,128)S(1)} all-to-all(f32[32,1,128]{2,1,0:T(1,128)} %bitcast.22), channel_id=1, replica_groups=mesh['dp'=8,'pipe'=4] {'pipe','dp'}, dimensions={0} | all-to-all | bytes 32768 | tf_op jit(solution)/shard_map/all_to_all | solution.py:492
  22.6 0.0 collective-permute-done.1.from_two.refs_2_
  22.6 0.0 collective-permute-start.4
  22.7 0.0 collective-permute-done.2.from_four.refs_3_
  22.7 0.5 %collective-permute-start.5 = (s32[2,2,2,9216]{3,2,1,0:T(2,128)S(1)}, s32[2,2,2,9216]{3,2,1,0:T(2,128)S(1)}, u32[]{:S(2)}, u32[]{:S(2)}) collective-permute-start(s32[2,2,2,9216]{3,2,1,0:T(2,128)S(1)} %collective-permute-done.2.from_four.refs_3_), channel_id=1, source_target_pairs={{0,4},{4,0},{8,12},{12,8},{16,20},{20,16},{24,28},{28,24},{1,5},{5... | collective-permute-start | bytes 884744 | tf_op jit(solution)/shard_map/ppermute | solution.py:484
  23.2 0.0 collective-permute-done.3.refs_4_
  23.2 0.1 collective-permute-start.6
  23.2 0.0 copy-done.2
  23.2 0.0 copy-done.3
  23.2 0.0 copy-done
  23.2 1.2 %base.1 = f32[16,8320]{1,0:T(8,128)S(1)} custom-call(s32[4,128]{1,0:T(4,128)S(1)} %copy-done.2, s32[2,4]{1,0:T(2,128)S(1)} %bitcast.17, bf16[128,8192]{1,0:T(8,128)(2,1)S(1)} %bitcast.14, s32[2,2,12288]{2,1,0:T(2,128)S(1)} %collective-permute-done.from_one.refs_1_, s32[2,2,2,9216]{3,2,1,0:T(2,128)S(1)} %collective-permute-done.1.from_two.refs_2_, ...), custom_call_target="tpu_custom_call" | custom-call | tf_op jit(solution)/shard_map/base/pallas_call | solution.py:498
  24.4 0.0 collective-permute-done.4.refs_5_
  24.4 0.2 collective-permute-done.5.refs_6_
  24.6 0.4 %collective-permute-done.6.refs_7_ = s32[2,2,2,8192]{3,2,1,0:T(2,128)S(1)} collective-permute-done((s32[2,2,2,8192]{3,2,1,0:T(2,128)S(1)}, s32[2,2,2,8192]{3,2,1,0:T(2,128)S(1)}, u32[]{:S(2)}, u32[]{:S(2)}) %collective-permute-start.6) | collective-permute-done | bytes 262176 | tf_op jit(solution)/shard_map/ppermute | solution.py:484
  25.0 0.0 copy-done.1
  25.0 2.9 %update.1 = (f32[16,8192]{1,0:T(8,128)}, f32[16,8192]{1,0:T(8,128)}, f32[16,8192]{1,0:T(8,128)}) custom-call(f32[32,128]{1,0:T(8,128)S(1)} %bitcast.15, f32[16,8320]{1,0:T(8,128)S(1)} %base.1, s32[2,2,8192]{2,1,0:T(2,128)S(1)} %copy-done.1, s32[2,2,12288]{2,1,0:T(2,128)S(1)} %collective-permute-done.from_one.refs_1_, ...), custom_call_target="tpu_custom_call" | custom-call | tf_op jit(solution)/shard_map/update/pallas_call | solution.py:514
Async XLA Ops:
  0.6 22.6 %copy-start.2 = (s32[4,128]{1,0:T(4,128)S(1)}, s32[4,128]{1,0:T(4,128)}, u32[]{:S(2)}) copy-start(s32[4,128]{1,0:T(4,128)} %dest.3) | copy-start | bytes 6148
  0.6 22.6 %copy-start.3 = (s32[4,2]{0,1:T(2,128)S(1)}, s32[4,2]{0,1:T(2,128)}, u32[]{:S(2)}) copy-start(s32[4,2]{0,1:T(2,128)} %param.14) | copy-start | bytes 100
  0.7 22.6 %copy-start = (bf16[1,1,128,8192]{3,2,1,0:T(8,128)(2,1)S(1)}, bf16[1,1,128,8192]{3,2,1,0:T(8,128)(2,1)}, u32[]{:S(2)}) copy-start(bf16[1,1,128,8192]{3,2,1,0:T(8,128)(2,1)} %param.13) | copy-start | bytes 6291460
  4.4 20.6 %copy-start.1 = (s32[2,2,8192]{2,1,0:T(2,128)S(1)}, s32[2,2,8192]{2,1,0:T(2,128)}, u32[]{:S(2)}) copy-start(s32[2,2,8192]{2,1,0:T(2,128)} %get-tuple-element.20.refs_0_) | copy-start | bytes 393220
  4.4 4.6 %collective-permute-start = (s32[2,2,12288]{2,1,0:T(2,128)}, s32[2,2,12288]{2,1,0:T(2,128)S(1)}, u32[]{:S(2)}, u32[]{:S(2)}) collective-permute-start(s32[2,2,12288]{2,1,0:T(2,128)} %get-tuple-element.17), channel_id=1, source_target_pairs={{0,4},{4,0},{8,12},{12,8},{16,20},{20,16},{24,28},{28,24},{1,5},{5... | collective-permute-start | bytes 589832 | tf_op jit(solution)/shard_map/ppermute | solution.py:484
  4.9 17.7 %collective-permute-start.1 = (s32[2,2,2,9216]{3,2,1,0:T(2,128)}, s32[2,2,2,9216]{3,2,1,0:T(2,128)S(1)}, u32[]{:S(2)}, u32[]{:S(2)}) collective-permute-start(s32[2,2,2,9216]{3,2,1,0:T(2,128)} %get-tuple-element.18), channel_id=1, source_target_pairs={{0,8},{4,12},{8,0},{12,4},{16,24},{20,28},{24,16},{28,20},{1,9},{5... | collective-permute-start | bytes 884744 | tf_op jit(solution)/shard_map/ppermute | solution.py:484
  7.5 15.2 %collective-permute-start.2 = (s32[2,2,2,9216]{3,2,1,0:T(2,128)}, s32[2,2,2,9216]{3,2,1,0:T(2,128)S(1)}, u32[]{:S(2)}, u32[]{:S(2)}) collective-permute-start(s32[2,2,2,9216]{3,2,1,0:T(2,128)} %get-tuple-element.19), channel_id=1, source_target_pairs={{0,16},{4,20},{8,24},{12,28},{16,0},{20,4},{24,8},{28,12},{1,17},{... | collective-permute-start | bytes 884744 | tf_op jit(solution)/shard_map/ppermute | solution.py:484
  9.0 14.1 %collective-permute-start.3 = (s32[2,2,2,8192]{3,2,1,0:T(2,128)}, s32[2,2,2,8192]{3,2,1,0:T(2,128)S(1)}, u32[]{:S(2)}, u32[]{:S(2)}) collective-permute-start(s32[2,2,2,8192]{3,2,1,0:T(2,128)} %get-tuple-element.22), channel_id=1, source_target_pairs={{0,24},{4,28},{8,16},{12,20},{16,8},{20,12},{24,0},{28,4},{1,25},{... | collective-permute-start | bytes 786440 | tf_op jit(solution)/shard_map/ppermute | solution.py:484
  22.6 1.8 %collective-permute-start.4 = (s32[2,2,2,9216]{3,2,1,0:T(2,128)S(1)}, s32[2,2,2,9216]{3,2,1,0:T(2,128)S(1)}, u32[]{:S(2)}, u32[]{:S(2)}) collective-permute-start(s32[2,2,2,9216]{3,2,1,0:T(2,128)S(1)} %collective-permute-done.1.from_two.refs_2_), channel_id=1, source_target_pairs={{0,4},{4,0},{8,12},{12,8},{16,20},{20,16},{24,28},{28,24},{1,5},{5... | collective-permute-start | bytes 884744 | tf_op jit(solution)/shard_map/ppermute | solution.py:484
  22.7 2.0 %collective-permute-start.5 = (s32[2,2,2,9216]{3,2,1,0:T(2,128)S(1)}, s32[2,2,2,9216]{3,2,1,0:T(2,128)S(1)}, u32[]{:S(2)}, u32[]{:S(2)}) collective-permute-start(s32[2,2,2,9216]{3,2,1,0:T(2,128)S(1)} %collective-permute-done.2.from_four.refs_3_), channel_id=1, source_target_pairs={{0,4},{4,0},{8,12},{12,8},{16,20},{20,16},{24,28},{28,24},{1,5},{5... | collective-permute-start | bytes 884744 | tf_op jit(solution)/shard_map/ppermute | solution.py:484
  23.2 1.9 %collective-permute-start.6 = (s32[2,2,2,8192]{3,2,1,0:T(2,128)S(1)}, s32[2,2,2,8192]{3,2,1,0:T(2,128)S(1)}, u32[]{:S(2)}, u32[]{:S(2)}) collective-permute-start(s32[2,2,2,8192]{3,2,1,0:T(2,128)S(1)} %collective-permute-done.3.refs_4_), channel_id=1, source_target_pairs={{0,4},{4,0},{8,12},{12,8},{16,20},{20,16},{24,28},{28,24},{1,5},{5... | collective-permute-start | bytes 786440 | tf_op jit(solution)/shard_map/ppermute | solution.py:484

commit v6 on v5

--- a/solution.py
+++ b/solution.py
@@ -460,7 +460,7 @@
     packed = pl.pallas_call(
         functools.partial(pack_kernel, ranks, cap, fails, devices),
         out_shape=[jax.ShapeDtypeStruct(payload_shape(k, cap, width), i32) for k in kinds]
-        + [jax.ShapeDtypeStruct((devices, 128), f32)],
+        + [pltpu.VMEM((devices, 128), f32)],
         in_specs=[ANY] * 8,
         out_specs=[ANY] * (len(kinds) + 1),
         scratch_shapes=[

time: 28.1 us -> 28.1 us (level)
  no operation moved by 1% of the time
where the time goes in v6:
time: 28.1 us; the launch traced here: 28 us
  blocking collectives  12.6 us (45%)
  Pallas kernels  7.87 us (28%)
  starting transfers between devices  6.19 us (22%)
  between operations  0.7 us (2%)
  waiting for transfers between devices  0.6 us (2%)
    all_to_all x1, blocking collectives, local(): lax.all_to_all(total, ('pipe', 'dp'), split_axis=0, concat_axis=0, tiled=...  12.6 us
    ppermute x7, starting transfers between devices, send(): return lax.ppermute(value, 'dp', [(i, i ^ k) for i in range(ranks)])  6.19 us
    pallas_call x1, Pallas kernels, local(): pl.pallas_call(functools.partial(pack_kernel, ranks, cap, fails, devices)...  3.76 us
    pallas_call x1, Pallas kernels, local(): pl.pallas_call(functools.partial(update_kernel, ranks, cap, devices * row...  2.93 us
    pallas_call x1, Pallas kernels, local(): pl.pallas_call(functools.partial(base_kernel, ranks, cap, fails), out_sha...  1.17 us
    ppermute x7, waiting for transfers between devices, send(): return lax.ppermute(value, 'dp', [(i, i ^ k) for i in range(ranks)])  0.6 us
  transfers between devices with their start and end apart: 7, of which 2 were waited for; matrix products, arithmetic and copies ran while one was open for 0% of the time, Pallas kernels for 4%

profile of v6, /device:TPU:0, one launch (start us, length us, event | category | flops | bytes accessed | tf_op | source)
XLA Modules:
  0.0 28.0 jit_solution(334401987360310378)
XLA Ops:
  0.6 0.0 copy-start.2
  0.6 0.0 copy-start.3
  0.7 0.0 copy-start
  0.7 3.8 %pack.1 = (s32[2,2,8192]{2,1,0:T(2,128)}, s32[2,2,12288]{2,1,0:T(2,128)}, s32[2,2,2,9216]{3,2,1,0:T(2,128)}, s32[2,2,2,9216]{3,2,1,0:T(2,128)}, s32[2,2,2,8192]{3,2,1,0:T(2,128)}, /*index=5*/f32[32,128]{1,0:T(8,128)S(1)}) custom-call(s32[4,128]{1,0:T(4,128)} %dest.3, s32[2,4]{1,0:T(2,128)} %bitcast.17, s32[1,16]{1,0:T(1,128)} %grad_exponent.1, ...), custom_call_target="tpu_custom_call" | custom-call | tf_op jit(solution)/shard_map/pack/pallas_call | solution.py:460
  4.4 0.0 copy-start.1
  4.4 0.5 %collective-permute-start = (s32[2,2,12288]{2,1,0:T(2,128)}, s32[2,2,12288]{2,1,0:T(2,128)S(1)}, u32[]{:S(2)}, u32[]{:S(2)}) collective-permute-start(s32[2,2,12288]{2,1,0:T(2,128)} %get-tuple-element.17), channel_id=1, source_target_pairs={{0,4},{4,0},{8,12},{12,8},{16,20},{20,16},{24,28},{28,24},{1,5},{5... | collective-permute-start | bytes 589832 | tf_op jit(solution)/shard_map/ppermute | solution.py:484
  5.0 2.6 %collective-permute-start.1 = (s32[2,2,2,9216]{3,2,1,0:T(2,128)}, s32[2,2,2,9216]{3,2,1,0:T(2,128)S(1)}, u32[]{:S(2)}, u32[]{:S(2)}) collective-permute-start(s32[2,2,2,9216]{3,2,1,0:T(2,128)} %get-tuple-element.18), channel_id=1, source_target_pairs={{0,8},{4,12},{8,0},{12,4},{16,24},{20,28},{24,16},{28,20},{1,9},{5... | collective-permute-start | bytes 884744 | tf_op jit(solution)/shard_map/ppermute | solution.py:484
  7.5 1.5 %collective-permute-start.2 = (s32[2,2,2,9216]{3,2,1,0:T(2,128)}, s32[2,2,2,9216]{3,2,1,0:T(2,128)S(1)}, u32[]{:S(2)}, u32[]{:S(2)}) collective-permute-start(s32[2,2,2,9216]{3,2,1,0:T(2,128)} %get-tuple-element.19), channel_id=1, source_target_pairs={{0,16},{4,20},{8,24},{12,28},{16,0},{20,4},{24,8},{28,12},{1,17},{... | collective-permute-start | bytes 884744 | tf_op jit(solution)/shard_map/ppermute | solution.py:484
  9.0 0.0 collective-permute-done.from_one.refs_1_
  9.0 1.0 %collective-permute-start.3 = (s32[2,2,2,8192]{3,2,1,0:T(2,128)}, s32[2,2,2,8192]{3,2,1,0:T(2,128)S(1)}, u32[]{:S(2)}, u32[]{:S(2)}) collective-permute-start(s32[2,2,2,8192]{3,2,1,0:T(2,128)} %get-tuple-element.22), channel_id=1, source_target_pairs={{0,24},{4,28},{8,16},{12,20},{16,8},{20,12},{24,0},{28,4},{1,25},{... | collective-permute-start | bytes 786440 | tf_op jit(solution)/shard_map/ppermute | solution.py:484
  10.1 12.6 %all_to_all.11 = f32[32,1,128]{2,1,0:T(1,128)S(1)} all-to-all(f32[32,1,128]{2,1,0:T(1,128)S(1)} %bitcast.16), channel_id=1, replica_groups=mesh['dp'=8,'pipe'=4] {'pipe','dp'}, dimensions={0} | all-to-all | bytes 32768 | tf_op jit(solution)/shard_map/all_to_all | solution.py:492
  22.7 0.0 collective-permute-done.1.from_two.refs_2_
  22.7 0.0 collective-permute-start.4
  22.7 0.0 collective-permute-done.2.from_four.refs_3_
  22.7 0.5 %collective-permute-start.5 = (s32[2,2,2,9216]{3,2,1,0:T(2,128)S(1)}, s32[2,2,2,9216]{3,2,1,0:T(2,128)S(1)}, u32[]{:S(2)}, u32[]{:S(2)}) collective-permute-start(s32[2,2,2,9216]{3,2,1,0:T(2,128)S(1)} %collective-permute-done.2.from_four.refs_3_), channel_id=1, source_target_pairs={{0,4},{4,0},{8,12},{12,8},{16,20},{20,16},{24,28},{28,24},{1,5},{5... | collective-permute-start | bytes 884744 | tf_op jit(solution)/shard_map/ppermute | solution.py:484
  23.2 0.0 collective-permute-done.3.refs_4_
  23.2 0.1 collective-permute-start.6
  23.3 0.0 copy-done.2
  23.3 0.0 copy-done.3
  23.3 0.0 copy-done
  23.3 1.2 %base.1 = f32[16,8320]{1,0:T(8,128)S(1)} custom-call(s32[4,128]{1,0:T(4,128)S(1)} %copy-done.2, s32[2,4]{1,0:T(2,128)S(1)} %bitcast.18, bf16[128,8192]{1,0:T(8,128)(2,1)S(1)} %bitcast.14, s32[2,2,12288]{2,1,0:T(2,128)S(1)} %collective-permute-done.from_one.refs_1_, s32[2,2,2,9216]{3,2,1,0:T(2,128)S(1)} %collective-permute-done.1.from_two.refs_2_, ...), custom_call_target="tpu_custom_call" | custom-call | tf_op jit(solution)/shard_map/base/pallas_call | solution.py:498
  24.4 0.0 collective-permute-done.4.refs_5_
  24.5 0.2 collective-permute-done.5.refs_6_
  24.7 0.4 %collective-permute-done.6.refs_7_ = s32[2,2,2,8192]{3,2,1,0:T(2,128)S(1)} collective-permute-done((s32[2,2,2,8192]{3,2,1,0:T(2,128)S(1)}, s32[2,2,2,8192]{3,2,1,0:T(2,128)S(1)}, u32[]{:S(2)}, u32[]{:S(2)}) %collective-permute-start.6) | collective-permute-done | bytes 262176 | tf_op jit(solution)/shard_map/ppermute | solution.py:484
  25.0 0.0 copy-done.1
  25.1 2.9 %update.1 = (f32[16,8192]{1,0:T(8,128)}, f32[16,8192]{1,0:T(8,128)}, f32[16,8192]{1,0:T(8,128)}) custom-call(f32[32,128]{1,0:T(8,128)S(1)} %bitcast.15, f32[16,8320]{1,0:T(8,128)S(1)} %base.1, s32[2,2,8192]{2,1,0:T(2,128)S(1)} %copy-done.1, s32[2,2,12288]{2,1,0:T(2,128)S(1)} %collective-permute-done.from_one.refs_1_, ...), custom_call_target="tpu_custom_call" | custom-call | tf_op jit(solution)/shard_map/update/pallas_call | solution.py:514
Async XLA Ops:
  0.6 22.6 %copy-start.2 = (s32[4,128]{1,0:T(4,128)S(1)}, s32[4,128]{1,0:T(4,128)}, u32[]{:S(2)}) copy-start(s32[4,128]{1,0:T(4,128)} %dest.3) | copy-start | bytes 6148
  0.6 22.6 %copy-start.3 = (s32[4,2]{0,1:T(2,128)S(1)}, s32[4,2]{0,1:T(2,128)}, u32[]{:S(2)}) copy-start(s32[4,2]{0,1:T(2,128)} %param.14) | copy-start | bytes 100
  0.7 22.6 %copy-start = (bf16[1,1,128,8192]{3,2,1,0:T(8,128)(2,1)S(1)}, bf16[1,1,128,8192]{3,2,1,0:T(8,128)(2,1)}, u32[]{:S(2)}) copy-start(bf16[1,1,128,8192]{3,2,1,0:T(8,128)(2,1)} %param.13) | copy-start | bytes 6291460
  4.4 20.6 %copy-start.1 = (s32[2,2,8192]{2,1,0:T(2,128)S(1)}, s32[2,2,8192]{2,1,0:T(2,128)}, u32[]{:S(2)}) copy-start(s32[2,2,8192]{2,1,0:T(2,128)} %get-tuple-element.20.refs_0_) | copy-start | bytes 393220
  4.4 4.6 %collective-permute-start = (s32[2,2,12288]{2,1,0:T(2,128)}, s32[2,2,12288]{2,1,0:T(2,128)S(1)}, u32[]{:S(2)}, u32[]{:S(2)}) collective-permute-start(s32[2,2,12288]{2,1,0:T(2,128)} %get-tuple-element.17), channel_id=1, source_target_pairs={{0,4},{4,0},{8,12},{12,8},{16,20},{20,16},{24,28},{28,24},{1,5},{5... | collective-permute-start | bytes 589832 | tf_op jit(solution)/shard_map/ppermute | solution.py:484
  5.0 17.7 %collective-permute-start.1 = (s32[2,2,2,9216]{3,2,1,0:T(2,128)}, s32[2,2,2,9216]{3,2,1,0:T(2,128)S(1)}, u32[]{:S(2)}, u32[]{:S(2)}) collective-permute-start(s32[2,2,2,9216]{3,2,1,0:T(2,128)} %get-tuple-element.18), channel_id=1, source_target_pairs={{0,8},{4,12},{8,0},{12,4},{16,24},{20,28},{24,16},{28,20},{1,9},{5... | collective-permute-start | bytes 884744 | tf_op jit(solution)/shard_map/ppermute | solution.py:484
  7.5 15.2 %collective-permute-start.2 = (s32[2,2,2,9216]{3,2,1,0:T(2,128)}, s32[2,2,2,9216]{3,2,1,0:T(2,128)S(1)}, u32[]{:S(2)}, u32[]{:S(2)}) collective-permute-start(s32[2,2,2,9216]{3,2,1,0:T(2,128)} %get-tuple-element.19), channel_id=1, source_target_pairs={{0,16},{4,20},{8,24},{12,28},{16,0},{20,4},{24,8},{28,12},{1,17},{... | collective-permute-start | bytes 884744 | tf_op jit(solution)/shard_map/ppermute | solution.py:484
  9.0 14.1 %collective-permute-start.3 = (s32[2,2,2,8192]{3,2,1,0:T(2,128)}, s32[2,2,2,8192]{3,2,1,0:T(2,128)S(1)}, u32[]{:S(2)}, u32[]{:S(2)}) collective-permute-start(s32[2,2,2,8192]{3,2,1,0:T(2,128)} %get-tuple-element.22), channel_id=1, source_target_pairs={{0,24},{4,28},{8,16},{12,20},{16,8},{20,12},{24,0},{28,4},{1,25},{... | collective-permute-start | bytes 786440 | tf_op jit(solution)/shard_map/ppermute | solution.py:484
  22.7 1.8 %collective-permute-start.4 = (s32[2,2,2,9216]{3,2,1,0:T(2,128)S(1)}, s32[2,2,2,9216]{3,2,1,0:T(2,128)S(1)}, u32[]{:S(2)}, u32[]{:S(2)}) collective-permute-start(s32[2,2,2,9216]{3,2,1,0:T(2,128)S(1)} %collective-permute-done.1.from_two.refs_2_), channel_id=1, source_target_pairs={{0,4},{4,0},{8,12},{12,8},{16,20},{20,16},{24,28},{28,24},{1,5},{5... | collective-permute-start | bytes 884744 | tf_op jit(solution)/shard_map/ppermute | solution.py:484
  22.7 2.0 %collective-permute-start.5 = (s32[2,2,2,9216]{3,2,1,0:T(2,128)S(1)}, s32[2,2,2,9216]{3,2,1,0:T(2,128)S(1)}, u32[]{:S(2)}, u32[]{:S(2)}) collective-permute-start(s32[2,2,2,9216]{3,2,1,0:T(2,128)S(1)} %collective-permute-done.2.from_four.refs_3_), channel_id=1, source_target_pairs={{0,4},{4,0},{8,12},{12,8},{16,20},{20,16},{24,28},{28,24},{1,5},{5... | collective-permute-start | bytes 884744 | tf_op jit(solution)/shard_map/ppermute | solution.py:484
  23.2 1.9 %collective-permute-start.6 = (s32[2,2,2,8192]{3,2,1,0:T(2,128)S(1)}, s32[2,2,2,8192]{3,2,1,0:T(2,128)S(1)}, u32[]{:S(2)}, u32[]{:S(2)}) collective-permute-start(s32[2,2,2,8192]{3,2,1,0:T(2,128)S(1)} %collective-permute-done.3.refs_4_), channel_id=1, source_target_pairs={{0,4},{4,0},{8,12},{12,8},{16,20},{20,16},{24,28},{28,24},{1,5},{5... | collective-permute-start | bytes 786440 | tf_op jit(solution)/shard_map/ppermute | solution.py:484
